TPU v7x, 768 devices: a whole 4x8x12 slice. The times are simulated.
768 devices in a mesh: emb: 32 (over y_hi, x, core), dense: 24 (over z, y_lo).
Axes of the slice: x: 4, y: 8 (y_hi: 4, y_lo: 2; y = y_hi * 2 + y_lo), z: 12, core: 2. Of those that a mesh axis runs over, the one named last changes fastest.
Arguments:
- pooled: bfloat16 [18432, 3328], P('dense'), may hold values from -6 to 6
- upstream: bfloat16 [18432, 4096], P('dense', 'emb'), may hold values from -6 to 6
- preact: bfloat16 [18432, 4096], P('dense', 'emb'), may hold values from -6 to 6
- tower_w: bfloat16 [3328, 4096], P(None, 'emb'), may hold values from -0.109375 to 0.109375
- row_ids: int32 [18432, 26], P('dense'), may hold values from 0 to 65535, as said below
- table: float32 [65536, 128], P('emb'), may hold values from -4 to 4
- accum: float32 [65536], P('emb'), may hold values from 0.01 to 1
Outputs:
- weight_grad: float32 [3328, 4096], P(None, 'emb')
- bias_grad: float32 [4096], P('emb')
- new_table: float32 [65536, 128], P('emb')
- new_accum: float32 [65536], P('emb')
Inputs may be any that keep to these rules, and one draw needn't show every extreme that they name: `row_ids`: row r is owned by index r // 2048 of emb. In each aligned block of 24 samples (the samples of one device, taken in order with dense as the slower index), at most 40 of the block's entries name rows of any one owner, and exactly 40 name rows of some owner.
All inputs are finite; a program needn't handle non-finite values.
Results may differ from a plain program's by a relative error of at most 0.007.
Values sent between devices are 32-bit elements; how exact they have to be, the bound alone decides.
A program may use at most 64 MiB of HBM per device.

v0:
```python
import jax
import jax.numpy as jnp
from jax import lax
from jax.sharding import PartitionSpec as P

learn_rate = 0.5
highest = lax.Precision.HIGHEST


def silu_slope(preact_f):
    sigmoid_val = jax.nn.sigmoid(preact_f)
    return sigmoid_val * (1.0 + preact_f * (1.0 - sigmoid_val))


def shards(pooled, upstream, preact, tower_w, row_ids, table, accum):
    slope = silu_slope(preact.astype(jnp.float32))
    deltas = (upstream.astype(jnp.float32) * slope).astype(jnp.bfloat16)
    emb_count = lax.axis_size("emb")
    sample_rows = deltas.shape[0] // emb_count
    width_e = table.shape[1]
    local_rows = table.shape[0]
    weight_grad = lax.dot_general(
        pooled, deltas, (((0,), (0,)), ((), ())), preferred_element_type=jnp.float32
    )
    bias_grad = jnp.sum(deltas.astype(jnp.float32), axis=0)
    weight_grad, bias_grad = lax.psum((weight_grad, bias_grad), "dense")
    pooled_grad = lax.psum_scatter(
        lax.dot_general(
            deltas, tower_w, (((1,), (1,)), ((), ())), preferred_element_type=jnp.float32
        ),
        "emb",
        scatter_dimension=0,
        tiled=True,
    )
    mine = lax.axis_index("emb")
    block_ids = lax.dynamic_slice_in_dim(row_ids, mine * sample_rows, sample_rows, 0).reshape(-1)
    owners = block_ids // local_rows
    offsets = block_ids % local_rows
    entries = block_ids.shape[0]
    capacity = 2 * ((entries + emb_count - 1) // emb_count)
    member = (owners[:, None] == jnp.arange(emb_count, dtype=jnp.int32)[None, :]).astype(
        jnp.float32
    )
    before = (
        jnp.arange(entries, dtype=jnp.int32)[None, :]
        < jnp.arange(entries, dtype=jnp.int32)[:, None]
    ).astype(jnp.float32)
    prior = jnp.dot(before, member, precision=highest, preferred_element_type=jnp.float32)
    ranks = jnp.sum(prior * member, axis=1).astype(jnp.int32)
    slot_of = owners * capacity + ranks
    total_slots = emb_count * capacity
    placing = (jnp.arange(total_slots, dtype=jnp.int32)[:, None] == slot_of[None, :]).astype(
        jnp.float32
    )
    grad_rows = pooled_grad.reshape(entries, width_e)
    send_rows = jnp.dot(placing, grad_rows, precision=highest, preferred_element_type=jnp.float32)
    filled = jnp.sum(placing, axis=1) > 0.5
    placed_offsets = jnp.dot(
        placing, offsets.astype(jnp.float32), precision=highest, preferred_element_type=jnp.float32
    )
    send_slots = jnp.where(filled, placed_offsets.astype(jnp.int32), local_rows)
    send_rows = send_rows.reshape(emb_count, capacity, width_e)
    send_slots = send_slots.reshape(emb_count, capacity)
    got_rows, got_slots = (
        lax.all_to_all(send_rows, "emb", split_axis=0, concat_axis=0, tiled=True),
        lax.all_to_all(send_slots, "emb", split_axis=0, concat_axis=0, tiled=True),
    )
    landing = (
        jnp.arange(local_rows, dtype=jnp.int32)[:, None] == got_slots.reshape(-1)[None, :]
    ).astype(jnp.float32)
    row_grad = jnp.dot(
        landing,
        got_rows.reshape(-1, width_e),
        precision=highest,
        preferred_element_type=jnp.float32,
    )
    row_grad = lax.psum(row_grad, "dense")
    new_accum = accum + jnp.mean(row_grad * row_grad, axis=1)
    new_table = table - learn_rate * row_grad / jnp.sqrt(new_accum)[:, None]
    return (weight_grad, bias_grad, new_table, new_accum)


def solution(mesh):
    placed = (
        P("dense", None),
        P("dense", "emb"),
        P("dense", "emb"),
        P(None, "emb"),
        P("dense", None),
        P("emb", None),
        P("emb"),
    )
    return jax.shard_map(
        shards,
        mesh=mesh,
        in_specs=placed,
        out_specs=(P(None, "emb"), P("emb"), P("emb", None), P("emb")),
        check_vma=False,
    )
```

profile of v0, /device:TPU:2, one launch (start us, length us, event | category | flops | bytes accessed | tf_op | source)
XLA Modules:
  0.0 433.6 jit_solution(11334359372983806729)
XLA Ops:
  7.2 0.0 copy-start
  7.2 0.0 reduce-scatter.2.cloned.1.call-start
  7.2 1.3 convert_reduce_fusion.1
  8.5 0.0 copy-done
  8.5 5.4 %fusion.25 = f32[768,3328]{1,0:T(8,128)} fusion(bf16[768,128]{1,0:T(8,128)(2,1)S(1)} %get-tuple-element.21, bf16[3328,128]{1,0:T(8,128)(2,1)S(1)} %copy-done), kind=kOutput, calls=%fused_computation.46 | convolution fusion | flops 654311424 | bytes 11272192 | tf_op jit(solution)/shard_map/dot_general | solution.py:28
  13.9 0.0 reduce-scatter.2.cloned.1.call-update
  13.9 0.8 constant_dynamic-slice_fusion
  14.8 0.1 copy.14
  14.8 0.1 reshape.104
  15.0 0.3 fusion.10
  15.3 1.0 fusion.11
  16.3 0.4 convert_reduce_fusion
  16.7 0.7 all_to_all.9
  17.4 13.0 %all-to-all-start = ((s32[32,1,40]{2,1,0:T(1,128)}), s32[32,1,40]{2,1,0:T(1,128)S(1)}, u32[]{:S(2)}, u32[]{:S(2)}) async-start(s32[32,1,40]{2,1,0:T(1,128)} %all_to_all.9), calls=%async_computation | async-start | bytes 32768 | tf_op jit(solution)/shard_map/all_to_all | solution.py:66
  30.5 136.1 %reduce-scatter.2.cloned.1.call-done = f32[24,3328]{1,0:T(8,128)} async-done(((f32[768,3328]{1,0:T(8,128)}), f32[24,3328]{1,0:T(8,128)}) %reduce-scatter.2.cloned.1.call-update) | async-done | bytes 319504 | tf_op jit(solution)/shard_map/reduce_scatter | solution.py:27
  166.6 1.0 reshape.109
  167.6 2.4 fusion.2
  170.0 0.0 all-to-all-done
  170.0 7.5 %all-to-all-start.1 = ((f32[32,40,128]{2,1,0:T(8,128)}), f32[32,40,128]{2,1,0:T(8,128)S(1)}, u32[]{:S(2)}, u32[]{:S(2)}) async-start(f32[32,40,128]{2,1,0:T(8,128)} %fusion.2), calls=%async_computation.2 | async-start | bytes 1310720 | tf_op jit(solution)/shard_map/all_to_all | solution.py:65
  177.5 0.0 all-reduce.3.cloned.1.call-start
  177.5 4.5 %convolution_bitcast_fusion = f32[3328,128]{0,1:T(8,128)} fusion(bf16[768,128]{1,0:T(8,128)(2,1)S(1)} %get-tuple-element.21, bf16[768,3328]{1,0:T(8,128)(2,1)} %param.7), kind=kOutput, calls=%fused_computation.3 | convolution fusion | flops 654311424 | bytes 7012352 | tf_op jit(solution)/shard_map/dot_general | solution.py:22
  182.0 0.5 broadcast.104
  182.6 0.7 reduce.5
  183.3 0.1 eq.67
  183.3 13.0 %all-to-all-done.1 = f32[32,40,128]{2,1,0:T(8,128)S(1)} async-done(((f32[32,40,128]{2,1,0:T(8,128)}), f32[32,40,128]{2,1,0:T(8,128)S(1)}, u32[]{:S(2)}, u32[]{:S(2)}) %all-to-all-start.1) | async-done | bytes 655392 | tf_op jit(solution)/shard_map/all_to_all | solution.py:65
  196.3 5.7 %fusion = f32[2048,128]{1,0:T(8,128)} fusion(f32[1280,128]{1,0:T(8,128)S(1)} %bitcast.10, s32[1280]{0:T(1024)S(1)} %eq.67), kind=kOutput, calls=%fused_computation.1 | convolution fusion | flops 4029153280 | bytes 1709056 | tf_op jit(solution)/shard_map/dot_general | solution.py:71
  202.0 0.0 copy-start.3
  202.0 0.0 copy-start.2
  202.0 0.0 all-reduce.3.cloned.1.call-update
  202.1 52.8 %psum.22 = f32[128]{0:T(128)} all-reduce(f32[128]{0:T(128)S(1)} %get-tuple-element.20), channel_id=1, replica_groups=mesh['emb'=32,'dense'=24] {'dense'}, use_global_device_ids=true, to_apply=%region_2.0 | all-reduce | flops 128 | bytes 1024 | tf_op jit(solution)/shard_map/psum | solution.py:26
  254.9 165.6 %all-reduce.3.cloned.1.call-done = (f32[3328,128]{0,1:T(8,128)}, f32[2048,128]{1,0:T(8,128)}) async-done(((f32[3328,128]{0,1:T(8,128)}, f32[2048,128]{1,0:T(8,128)}), (f32[3328,128]{0,1:T(8,128)}, f32[2048,128]{1,0:T(8,128)})) %all-reduce.3.cloned.1.call-update) | async-done | bytes 2752528 | tf_op jit(solution)/shard_map/psum | solution.py:26
  420.5 0.0 copy-start.1
  420.5 1.7 multiply_reduce_fusion
  422.1 2.7 copy.15
  424.8 0.0 copy-done.3
  424.8 0.6 fusion.23
  425.4 0.0 copy-done.2
  425.4 0.0 copy-done.1
  425.4 1.3 divide_subtract_fusion
  (5 shorter events, 0.0 us)
Async XLA Ops:
  7.2 1.3 copy-start
  7.2 159.4 %reduce-scatter.2.cloned.1.call-start = ((), (), s32[]{:S(2)}) async-start(), calls=%async_computation.3 | async-start | bytes 10543104 | tf_op jit(solution)/shard_map/reduce_scatter | solution.py:27
  17.4 152.6 %all-to-all-start = ((s32[32,1,40]{2,1,0:T(1,128)}), s32[32,1,40]{2,1,0:T(1,128)S(1)}, u32[]{:S(2)}, u32[]{:S(2)}) async-start(s32[32,1,40]{2,1,0:T(1,128)} %all_to_all.9), calls=%async_computation | async-start | bytes 32768 | tf_op jit(solution)/shard_map/all_to_all | solution.py:66
  170.0 26.4 %all-to-all-start.1 = ((f32[32,40,128]{2,1,0:T(8,128)}), f32[32,40,128]{2,1,0:T(8,128)S(1)}, u32[]{:S(2)}, u32[]{:S(2)}) async-start(f32[32,40,128]{2,1,0:T(8,128)} %fusion.2), calls=%async_computation.2 | async-start | bytes 1310720 | tf_op jit(solution)/shard_map/all_to_all | solution.py:65
  177.5 243.0 %all-reduce.3.cloned.1.call-start = ((), (), s32[]{:S(2)}) async-start(), calls=%async_computation.4 | async-start | bytes 5505024 | tf_op jit(solution)/shard_map/psum | solution.py:26
  202.0 222.8 %copy-start.3 = (f32[2048]{0:T(1024)S(1)}, f32[2048]{0:T(1024)}, u32[]{:S(2)}) copy-start(f32[2048]{0:T(1024)} %param.13) | copy-start | bytes 24580
  202.0 223.4 %copy-start.2 = (f32[2048,128]{1,0:T(8,128)S(1)}, f32[2048,128]{1,0:T(8,128)}, u32[]{:S(2)}) copy-start(f32[2048,128]{1,0:T(8,128)} %param.12) | copy-start | bytes 3145732
  420.5 4.9 %copy-start.1 = (f32[2048,128]{1,0:T(8,128)S(1)}, f32[2048,128]{1,0:T(8,128)}, u32[]{:S(2)}) copy-start(f32[2048,128]{1,0:T(8,128)} %get-tuple-element.17) | copy-start | bytes 3145732
Sparse Core Ops, SparseCore 0:
  14.0 152.4 reduce-scatter.1
  202.2 218.2 all-reduce.2
where the time goes:
time: 434 us
  waiting for transfers between devices  315 us (73%)
  blocking collectives  52.8 us (12%)
  starting transfers between devices  20.6 us (5%)
  matrix products  19.3 us (4%)
  between operations  14.2 us (3%)
  local copies, waits for them, and re-layouts  6 us (1%)
  other arithmetic  5.96 us (1%)
    psum x1, waiting for transfers between devices, shards(): weight_grad, bias_grad = lax.psum((weight_grad, bias_grad), 'dense')  166 us
    reduce_scatter x1, waiting for transfers between devices, shards(): lax.psum_scatter(lax.dot_general(deltas, tower_w, (((1,), (1,)), ((), ())...  136 us
    psum x1, blocking collectives, shards(): weight_grad, bias_grad = lax.psum((weight_grad, bias_grad), 'dense')  52.8 us
    all_to_all x1, starting transfers between devices, shards(): lax.all_to_all(send_slots, 'emb', split_axis=0, concat_axis=0, tiled=True)  13 us
    all_to_all x1, waiting for transfers between devices, shards(): lax.all_to_all(send_rows, 'emb', split_axis=0, concat_axis=0, tiled=True)  13 us
  transfers between devices with their start and end apart: 4, of which 3 were waited for; matrix products, arithmetic and copies ran while one was open for 3% of the time, Pallas kernels for 0%

commit v1 on v0

v1 whole, which is shorter than its diff:
```python
import functools

import jax
import jax.numpy as jnp
from jax import lax
from jax.experimental import pallas as pl
from jax.experimental.pallas import tpu as pltpu
from jax.sharding import PartitionSpec as P

learn_rate = 0.5
MESH = pl.DeviceIdType.MESH
CHUNK = 256
CAP = 40
F32 = jnp.float32
BF16 = jnp.bfloat16


def silu_slope(preact_f):
    sigmoid_val = jax.nn.sigmoid(preact_f)
    return sigmoid_val * (1.0 + preact_f * (1.0 - sigmoid_val))


def remote(src, dst, send, recv, where):
    return pltpu.make_async_remote_copy(
        src_ref=src, dst_ref=dst, send_sem=send, recv_sem=recv, device_id=where, device_id_type=MESH
    )


def place_rows(ids, groups, local_rows):
    entries = ids.shape[1]
    owners = ids // local_rows
    member = (lax.broadcasted_iota(jnp.int32, (groups, entries), 0) == owners).astype(F32)
    earlier = (
        lax.broadcasted_iota(jnp.int32, (entries, entries), 0)
        < lax.broadcasted_iota(jnp.int32, (entries, entries), 1)
    ).astype(F32).astype(BF16)
    prior = jnp.dot(member.astype(BF16), earlier, preferred_element_type=F32)
    ranks = jnp.sum(prior * member, axis=0, keepdims=True).astype(jnp.int32)
    slot_of = owners * CAP + ranks
    return (
        (lax.broadcasted_iota(jnp.int32, (groups * CAP, entries), 0) == slot_of)
        .astype(F32)
        .astype(BF16)
    )


def halves(rows):
    high = rows.astype(BF16)
    low = (rows - high.astype(F32)).astype(BF16)
    return jnp.concatenate([high, low], axis=1)


def route_kernel(
    ny,
    nx,
    local_rows,
    deltas_ref,
    w_ref,
    ids_ref,
    got_ref,
    spread,
    give,
    take,
    w_give,
    w_take,
    left,
    right,
    part,
    relay,
    from_x,
    from_y,
    grads,
    placing,
    out_rows,
    in_rows,
    pair_send,
    pair_recv,
    w_send,
    w_recv,
    x_send,
    x_recv,
    y_send,
    y_recv,
    a_send,
    a_recv,
):
    chunks = part.shape[0]
    batch = deltas_ref.shape[0] // (ny * nx * 2)
    groups = ny * nx * 2
    me = lax.axis_index("emb")
    core = lax.rem(me, 2)
    at_x = lax.rem(me // 2, nx)
    at_y = me // (2 * nx)

    def there(y, x, c):
        return {"emb": (lax.rem(y, ny) * nx + lax.rem(x, nx)) * 2 + c}

    sibling = there(at_y, at_x, 1 - core)
    x_next = there(at_y, at_x + 1, core)
    x_prev = there(at_y, at_x + nx - 1, core)
    y_next = there(at_y + 1, at_x, core)
    y_prev = there(at_y + ny - 1, at_x, core)
    y_far = there(at_y + 2, at_x, core)

    barrier = pltpu.get_barrier_semaphore()

    def greet(k, carry):
        pl.semaphore_signal(
            barrier, inc=1, device_id={"emb": lax.rem(me + k, groups)}, device_id_type=MESH
        )
        return carry

    lax.fori_loop(1, groups, greet, 0)

    spread[...] = deltas_ref[...].astype(F32).reshape(groups, batch, 128)
    for q in range(nx):
        for p in range(ny):
            block = (lax.rem(at_y + p, ny) * nx + lax.rem(at_x + q, nx)) * 2
            give[q * ny + p] = spread[block + 1 - core]
            left[pl.ds((q * ny + p) * batch, batch), :] = spread[block + core]
    w_give[...] = w_ref[...].astype(F32).reshape(w_give.shape)
    right[:, :, :128] = w_ref[...].reshape(chunks, CHUNK, 128)
    pl.semaphore_wait(barrier, groups - 1)

    def pair_copy():
        return remote(give, take, pair_send, pair_recv, sibling)

    def w_copy(j):
        return remote(w_give.at[j], w_take.at[j], w_send.at[j], w_recv.at[j], sibling)

    half = 2 * batch

    def x_copy(j, kind):
        if kind == 0:
            src, dst, where = part.at[j, 2, pl.ds(0, half)], relay.at[j, 0], x_next
        elif kind == 1:
            src, dst, where = part.at[j, 2, pl.ds(half, half)], relay.at[j, 1], x_prev
        elif kind == 2:
            src, dst, where = part.at[j, 1], from_x.at[j, 0], x_next
        else:
            src, dst, where = part.at[j, 3], from_x.at[j, 1], x_prev
        return remote(src, dst, x_send.at[kind, j], x_recv.at[kind, j], where)

    def y_copy(j, kind):
        where = (y_next, y_far, y_prev)[kind]
        src = part.at[j, 0, pl.ds((kind + 1) * batch, batch)]
        return remote(src, from_y.at[j, kind], y_send.at[kind, j], y_recv.at[kind, j], where)

    pair_copy().start()

    def w_start(j, carry):
        w_copy(j).start()
        return carry

    lax.fori_loop(0, chunks, w_start, 0)
    pair_copy().wait_recv()
    left_own = left[...].astype(BF16)
    left_pair = take[...].reshape(left.shape).astype(BF16)

    def step(i, carry):
        @pl.when(i < chunks)
        def _():
            w_copy(i).wait_recv()
            right[i, :, 128:] = w_take[i].astype(BF16)
            product = lax.dot_general(
                jnp.concatenate([left_own, left_pair], axis=1),
                right[i],
                (((1,), (1,)), ((), ())),
                preferred_element_type=F32,
            )
            part[i] = product.reshape(part.shape[1:])
            x_copy(i, 0).start()
            x_copy(i, 1).start()

        @pl.when(jnp.logical_and(i >= 2, i < chunks + 2))
        def _():
            j = i - 2
            x_copy(j, 0).wait_recv()
            part[j, 1, pl.ds(0, half)] = part[j, 1, pl.ds(0, half)] + relay[j, 0]
            x_copy(j, 2).start()
            x_copy(j, 1).wait_recv()
            part[j, 3, pl.ds(half, half)] = part[j, 3, pl.ds(half, half)] + relay[j, 1]
            x_copy(j, 3).start()

        @pl.when(i == 3)
        def _():
            placing[...] = place_rows(ids_ref[...], groups, local_rows)

        @pl.when(jnp.logical_and(i >= 4, i < chunks + 4))
        def _():
            j = i - 4
            x_copy(j, 2).wait_recv()
            x_copy(j, 3).wait_recv()
            part[j, 0] = part[j, 0] + from_x[j, 0] + from_x[j, 1]
            for kind in (1, 0, 2):
                y_copy(j, kind).start()

        @pl.when(i >= 7)
        def _():
            j = i - 7
            for kind in range(3):
                y_copy(j, kind).wait_recv()
            total = part[j, 0, pl.ds(0, batch)] + from_y[j, 0] + from_y[j, 1] + from_y[j, 2]
            for n in range(CHUNK // 128):
                grads[j * (CHUNK // 128) + n] = total[:, n * 128 : (n + 1) * 128]

        return carry

    lax.fori_loop(0, chunks + 7, step, 0)

    wide = halves(grads[...].reshape(-1, 128))
    both = jnp.dot(placing[...], wide, preferred_element_type=F32)
    out_rows[...] = (both[:, :128] + both[:, 128:]).reshape(out_rows.shape)

    def a_copy(k):
        owner = lax.rem(me + k, groups)
        return remote(
            out_rows.at[owner], in_rows.at[me], a_send.at[k], a_recv.at[k], {"emb": owner}
        )

    def a_start(k, carry):
        a_copy(lax.rem(k + 14, groups - 1) + 1).start()
        return carry

    lax.fori_loop(1, groups, a_start, 0)
    in_rows[me] = out_rows[me]

    def drain(j, carry):
        w_copy(j).wait_send()
        for kind in range(4):
            x_copy(j, kind).wait_send()
        for kind in range(3):
            y_copy(j, kind).wait_send()
        return carry

    pair_copy().wait_send()
    lax.fori_loop(0, chunks, drain, 0)

    def a_wait(k, carry):
        a_copy(k).wait_recv()
        a_copy(k).wait_send()
        return carry

    lax.fori_loop(1, groups, a_wait, 0)
    got_ref[...] = in_rows[...]


def route(deltas, tower_w, block_ids, local_rows, ny, nx):
    samples = deltas.shape[0]
    groups = ny * nx * 2
    batch = samples // groups
    columns = tower_w.shape[0]
    chunks = columns // CHUNK
    entries = block_ids.shape[1]
    vmem = pltpu.VMEM
    dma = pltpu.SemaphoreType.DMA
    return pl.pallas_call(
        functools.partial(route_kernel, ny, nx, local_rows),
        out_shape=jax.ShapeDtypeStruct((groups, CAP, 128), F32),
        in_specs=[pl.BlockSpec(memory_space=vmem)] * 3,
        out_specs=pl.BlockSpec(memory_space=vmem),
        scratch_shapes=[
            vmem((groups, batch, 128), F32),
            vmem((nx * ny, batch, 128), F32),
            vmem((nx * ny, batch, 128), F32),
            vmem((chunks, CHUNK, 128), F32),
            vmem((chunks, CHUNK, 128), F32),
            vmem((nx * ny * batch, 128), F32),
            vmem((chunks, CHUNK, 256), BF16),
            vmem((chunks, nx, ny * batch, CHUNK), F32),
            vmem((chunks, 2, 2 * batch, CHUNK), F32),
            vmem((chunks, 2, ny * batch, CHUNK), F32),
            vmem((chunks, 3, batch, CHUNK), F32),
            vmem((columns // 128, batch, 128), F32),
            vmem((groups * CAP, entries), BF16),
            vmem((groups, CAP, 128), F32),
            vmem((groups, CAP, 128), F32),
            dma,
            dma,
            dma((chunks,)),
            dma((chunks,)),
            dma((4, chunks)),
            dma((4, chunks)),
            dma((3, chunks)),
            dma((3, chunks)),
            dma((groups,)),
            dma((groups,)),
        ],
        compiler_params=pltpu.CompilerParams(
            collective_id=0, has_side_effects=True, vmem_limit_bytes=44 << 20
        ),
        cost_estimate=pl.CostEstimate(flops=1 << 30, bytes_accessed=8 << 20, transcendentals=0),
    )(deltas, tower_w, block_ids)


def landing_rows(ids, mine, local_rows):
    blocks, entries = ids.shape
    owners = ids // local_rows
    member = (owners == mine).astype(F32)
    earlier = (
        lax.broadcasted_iota(jnp.int32, (entries, entries), 0)
        < lax.broadcasted_iota(jnp.int32, (entries, entries), 1)
    ).astype(F32).astype(BF16)
    prior = jnp.dot(member.astype(BF16), earlier, preferred_element_type=F32)
    ranks = jnp.where(member > 0.5, prior.astype(jnp.int32), -1)
    offsets = (ids - owners * local_rows + 1).astype(F32)
    slots = lax.broadcasted_iota(jnp.int32, (CAP, entries), 0)
    columns = []
    for block in range(blocks):
        hit = jnp.where(slots == ranks[block : block + 1], offsets[block : block + 1], 0.0)
        columns.append(jnp.sum(hit, axis=1, keepdims=True))
    return jnp.concatenate(columns, axis=0) - 1.0


def update_kernel(
    nz,
    local_rows,
    rows_ref,
    ids_ref,
    bias_ref,
    total_ref,
    landing,
    sums,
    swap,
    mixed,
    from_z,
    final,
    s_send,
    s_recv,
    z_send,
    z_recv,
    g_send,
    g_recv,
    f_send,
    f_recv,
):
    mine = lax.axis_index("emb")
    me = lax.axis_index("dense")
    at_y = lax.rem(me, 2)
    at_z = me // 2
    shard = sums.shape[1]
    partner = {"dense": at_z * 2 + 1 - at_y}

    def away(k):
        return lax.rem(at_z + k, nz)

    def peer(k):
        return {"dense": away(k) * 2 + at_y}

    barrier = pltpu.get_barrier_semaphore()

    def greet(k, carry):
        pl.semaphore_signal(barrier, inc=1, device_id=peer(k), device_id_type=MESH)
        return carry

    lax.fori_loop(1, nz, greet, 0)
    pl.semaphore_signal(barrier, inc=1, device_id=partner, device_id_type=MESH)

    slots = rows_ref.shape[0] * rows_ref.shape[1]
    target = jnp.broadcast_to(landing_rows(ids_ref[...], mine, local_rows), (slots, 128))
    target = target.T[0:1].astype(jnp.int32)
    landing[...] = (
        (lax.broadcasted_iota(jnp.int32, (local_rows, slots), 0) == target)
        .astype(F32)
        .astype(BF16)
    )
    wide = halves(rows_ref[...].reshape(slots, 128))
    both = jnp.dot(landing[...], wide, preferred_element_type=F32)
    row_grad = both[:, :128] + both[:, 128:]
    spare = 2 * nz * shard - local_rows
    extra = jnp.where(
        lax.broadcasted_iota(jnp.int32, (spare, 128), 0) == 0,
        jnp.broadcast_to(bias_ref[...], (spare, 128)),
        0.0,
    )
    row_grad = jnp.concatenate([row_grad, extra], axis=0)
    sums[...] = row_grad.reshape(sums.shape)
    pl.semaphore_wait(barrier, nz)

    def s_copy(k):
        return remote(
            sums.at[away(k) * 2 + 1 - at_y], swap.at[k], s_send.at[k], s_recv.at[k], partner
        )

    def z_copy(k):
        return remote(mixed.at[k], from_z.at[k], z_send.at[k], z_recv.at[k], peer(k))

    def g_copy(k):
        return remote(final.at[me], final.at[me], g_send.at[k], g_recv.at[k], peer(k))

    def f_copy(k):
        source = away(nz - k) * 2 + at_y
        return remote(final.at[source], final.at[source], f_send.at[k], f_recv.at[k], partner)

    order = sorted(range(nz), key=lambda k: -min(k, nz - k))
    for k in order:
        s_copy(k).start()
    for k in order:
        s_copy(k).wait_recv()
        mixed[k] = sums[away(k) * 2 + at_y] + swap[k]
        if k:
            z_copy(k).start()
    total = mixed[0]
    for k in order[::-1]:
        if k:
            z_copy(k).wait_recv()
            total = total + from_z[k]
    final[me] = total
    for k in order:
        if k:
            g_copy(k).start()
    f_copy(0).start()
    for k in order[::-1]:
        if k:
            g_copy(k).wait_recv()
            f_copy(k).start()
    for k in order[::-1]:
        f_copy(k).wait_recv()
    for k in order:
        s_copy(k).wait_send()
        f_copy(k).wait_send()
        if k:
            z_copy(k).wait_send()
            g_copy(k).wait_send()
    total_ref[...] = final[...]


def update(rows, ids, bias, local_rows, dense):
    nz = dense // 2
    groups = rows.shape[0]
    shard = -(-(local_rows + 8) // (dense * 8)) * 8
    vmem = pltpu.VMEM
    dma = pltpu.SemaphoreType.DMA
    total = pl.pallas_call(
        functools.partial(update_kernel, nz, local_rows),
        out_shape=jax.ShapeDtypeStruct((dense, shard, 128), F32),
        in_specs=[pl.BlockSpec(memory_space=vmem)] * 3,
        out_specs=pl.BlockSpec(memory_space=vmem),
        scratch_shapes=[
            vmem((local_rows, groups * CAP), BF16),
            vmem((dense, shard, 128), F32),
            vmem((nz, shard, 128), F32),
            vmem((nz, shard, 128), F32),
            vmem((nz, shard, 128), F32),
            vmem((dense, shard, 128), F32),
        ]
        + [dma((nz,))] * 8,
        compiler_params=pltpu.CompilerParams(
            collective_id=1, has_side_effects=True, vmem_limit_bytes=44 << 20
        ),
        cost_estimate=pl.CostEstimate(flops=1 << 30, bytes_accessed=8 << 20, transcendentals=0),
    )(rows, ids, bias)
    return total.reshape(dense * shard, 128)


def shards(pooled, upstream, preact, tower_w, row_ids, table, accum):
    groups = lax.axis_size("emb")
    dense = lax.axis_size("dense")
    local_rows = table.shape[0]
    slope = silu_slope(preact.astype(F32))
    deltas = (upstream.astype(F32) * slope).astype(BF16)
    weight_grad = lax.dot_general(
        pooled, deltas, (((0,), (0,)), ((), ())), preferred_element_type=F32
    )
    bias = jnp.sum(deltas.astype(F32), axis=0)[None, :]
    weight_grad = lax.psum(weight_grad, "dense")
    ids = row_ids.reshape(groups, -1, row_ids.shape[1]).transpose(0, 2, 1).reshape(groups, -1)
    block_ids = lax.dynamic_slice_in_dim(ids, lax.axis_index("emb"), 1, 0)
    rows = route(deltas, tower_w, block_ids, local_rows, 4, 4)
    total = update(rows, ids, bias, local_rows, dense)
    row_grad = total[:local_rows]
    bias_grad = total[local_rows]
    new_accum = accum + jnp.mean(row_grad * row_grad, axis=1)
    new_table = table - learn_rate * row_grad / jnp.sqrt(new_accum)[:, None]
    return (weight_grad, bias_grad, new_table, new_accum)


def solution(mesh):
    placed = (
        P("dense", None),
        P("dense", "emb"),
        P("dense", "emb"),
        P(None, "emb"),
        P("dense", None),
        P("emb", None),
        P("emb"),
    )
    return jax.shard_map(
        shards,
        mesh=mesh,
        in_specs=placed,
        out_specs=(P(None, "emb"), P("emb"), P("emb", None), P("emb")),
        check_vma=False,
    )
```

time: 434 us -> 258 us (0.59)
  the two profiles are of different devices: /device:TPU:2 before, /device:TPU:14 now
where the time goes in v1:
time: 258 us
  Pallas kernels  174 us (67%)
  waiting for transfers between devices  57.6 us (22%)
  between operations  14.1 us (5%)
  local copies, waits for them, and re-layouts  4.85 us (2%)
  matrix products  4.5 us (2%)
  other arithmetic  3.47 us (1%)
    pallas_call x1, Pallas kernels, route(): pl.pallas_call(functools.partial(route_kernel, ny, nx, local_rows), out_s...  92.7 us
    pallas_call x1, Pallas kernels, update(): pl.pallas_call(functools.partial(update_kernel, nz, local_rows), out_shap...  80.9 us
    psum x1, waiting for transfers between devices, shards(): weight_grad = lax.psum(weight_grad, 'dense')  57.6 us
  transfers between devices with their start and end apart: 1, of which 1 were waited for; matrix products, arithmetic and copies ran while one was open for 1% of the time, Pallas kernels for 67%

profile of v1, /device:TPU:14, one launch (start us, length us, event | category | flops | bytes accessed | tf_op | source)
XLA Modules:
  0.0 258.2 jit_solution(15597511264405221497)
XLA Ops:
  7.2 0.0 all-reduce.2.cloned.1.call-start
  7.2 1.2 convert_reduce_fusion
  8.4 4.5 %convolution_bitcast_fusion = f32[3328,128]{0,1:T(8,128)} fusion(bf16[768,128]{1,0:T(8,128)(2,1)S(1)} %get-tuple-element.15.deltas_ref, bf16[768,3328]{1,0:T(8,128)(2,1)} %param.7), kind=kOutput, calls=%fused_computation | convolution fusion | flops 654311424 | bytes 7012352 | tf_op jit(solution)/shard_map/dot_general | solution.py:462
  12.9 0.0 copy-start.2
  12.9 0.0 copy-start
  12.9 0.0 all-reduce.2.cloned.1.call-update
  13.0 0.9 copy-done.2
  13.8 0.3 reshape.18
  14.1 0.3 copy.13
  14.4 0.2 reshape.19.ids_ref
  14.6 0.0 copy-done
  14.6 92.7 %shard_map.102.rows_ref = f32[32,40,128]{2,1,0:T(8,128)S(1)} custom-call(bf16[768,128]{1,0:T(8,128)(2,1)S(1)} %get-tuple-element.15.deltas_ref, bf16[3328,128]{1,0:T(8,128)(2,1)S(1)} %copy-done, s32[1,624]{1,0:T(1,128)S(1)} %constant_dynamic-slice_fusion.ids_ref), custom_call_target="tpu_custom_call" | custom-call | flops 1073741824 | bytes 8388608 | tf_op jit(solution)/shard_map/pallas_call | solution.py:257
  107.4 0.0 copy-start.3
  107.4 0.0 copy-start.1
  107.4 80.9 %shard_map.103 = f32[24,88,128]{2,1,0:T(8,128)S(1)} custom-call(f32[32,40,128]{2,1,0:T(8,128)S(1)} %shard_map.102.rows_ref, s32[32,624]{1,0:T(8,128)S(1)} %reshape.19.ids_ref, f32[1,128]{1,0:T(1,128)S(1)} %bitcast.14), custom_call_target="tpu_custom_call" | custom-call | flops 1073741824 | bytes 8388608 | tf_op jit(solution)/shard_map/pallas_call | solution.py:434
  188.3 0.3 multiply_reduce_fusion
  188.7 0.5 slice_bitcast_fusion
  189.2 0.0 copy-done.3
  189.2 0.6 fusion.7
  189.8 0.0 copy-done.1
  189.8 1.3 divide_subtract_fusion
  191.1 57.6 %all-reduce.2.cloned.1.call-done = f32[3328,128]{0,1:T(8,128)} async-done(((f32[3328,128]{0,1:T(8,128)}), f32[3328,128]{0,1:T(8,128)}) %all-reduce.2.cloned.1.call-update) | async-done | bytes 1703952 | tf_op jit(solution)/shard_map/psum | solution.py:466
  248.7 2.7 %copy.14 = f32[3328,128]{1,0:T(8,128)} copy(f32[3328,128]{0,1:T(8,128)} %all-reduce.2.cloned.1.call-done) | data formatting | bytes 3407872
  (1 shorter events, 0.0 us)
Async XLA Ops:
  7.2 241.5 %all-reduce.2.cloned.1.call-start = ((), (), s32[]{:S(2)}) async-start(), calls=%async_computation | async-start | bytes 3407872 | tf_op jit(solution)/shard_map/psum | solution.py:466
  12.9 0.9 copy-start.2
  12.9 1.7 copy-start
  107.4 81.8 %copy-start.3 = (f32[2048]{0:T(1024)S(1)}, f32[2048]{0:T(1024)}, u32[]{:S(2)}) copy-start(f32[2048]{0:T(1024)} %param.13) | copy-start | bytes 24580
  107.4 82.4 %copy-start.1 = (f32[2048,128]{1,0:T(8,128)S(1)}, f32[2048,128]{1,0:T(8,128)}, u32[]{:S(2)}) copy-start(f32[2048,128]{1,0:T(8,128)} %param.12) | copy-start | bytes 3145732
Sparse Core Ops, SparseCore 0:
  13.1 235.5 all-reduce.1

commit v2 on v1

v2 whole, which is shorter than its diff:
```python
import functools

import jax
import jax.numpy as jnp
from jax import lax
from jax.experimental import pallas as pl
from jax.experimental.pallas import tpu as pltpu
from jax.sharding import PartitionSpec as P

learn_rate = 0.5
MESH = pl.DeviceIdType.MESH
CHUNK = 256
CAP = 40
F32 = jnp.float32
BF16 = jnp.bfloat16


def silu_slope(preact_f):
    sigmoid_val = jax.nn.sigmoid(preact_f)
    return sigmoid_val * (1.0 + preact_f * (1.0 - sigmoid_val))


def remote(src, dst, send, recv, where):
    return pltpu.make_async_remote_copy(
        src_ref=src, dst_ref=dst, send_sem=send, recv_sem=recv, device_id=where, device_id_type=MESH
    )


def place_rows(ids, groups, local_rows):
    entries = ids.shape[1]
    owners = ids // local_rows
    member = (lax.broadcasted_iota(jnp.int32, (groups, entries), 0) == owners).astype(F32)
    earlier = (
        lax.broadcasted_iota(jnp.int32, (entries, entries), 0)
        < lax.broadcasted_iota(jnp.int32, (entries, entries), 1)
    ).astype(F32).astype(BF16)
    prior = jnp.dot(member.astype(BF16), earlier, preferred_element_type=F32)
    ranks = jnp.sum(prior * member, axis=0, keepdims=True).astype(jnp.int32)
    slot_of = owners * CAP + ranks
    return (
        (lax.broadcasted_iota(jnp.int32, (groups * CAP, entries), 0) == slot_of)
        .astype(F32)
        .astype(BF16)
    )


def halves(rows):
    high = rows.astype(BF16)
    low = (rows - high.astype(F32)).astype(BF16)
    return jnp.concatenate([high, low], axis=1)


def landing_rows(ids, mine, local_rows):
    blocks, entries = ids.shape
    owners = ids // local_rows
    member = (owners == mine).astype(F32)
    earlier = (
        lax.broadcasted_iota(jnp.int32, (entries, entries), 0)
        < lax.broadcasted_iota(jnp.int32, (entries, entries), 1)
    ).astype(F32).astype(BF16)
    prior = jnp.dot(member.astype(BF16), earlier, preferred_element_type=F32)
    ranks = jnp.where(member > 0.5, prior.astype(jnp.int32), -1)
    offsets = (ids - owners * local_rows + 1).astype(F32)
    slots = lax.broadcasted_iota(jnp.int32, (CAP, entries), 0)
    columns = []
    for block in range(blocks):
        hit = jnp.where(slots == ranks[block : block + 1], offsets[block : block + 1], 0.0)
        columns.append(jnp.sum(hit, axis=1, keepdims=True))
    return jnp.concatenate(columns, axis=0) - 1.0


def step_kernel(
    ny,
    nx,
    nz,
    local_rows,
    deltas_ref,
    w_ref,
    mine_ref,
    ids_ref,
    wg_ref,
    bias_ref,
    total_ref,
    tower_ref,
    spread,
    give,
    take,
    w_give,
    w_take,
    left,
    right,
    part,
    relay,
    from_x,
    from_y,
    grads,
    placing,
    out_rows,
    in_rows,
    target,
    landing,
    sums,
    swap,
    mixed,
    from_z,
    final,
    tower,
    t_from,
    t_swap,
    t_final,
    pair_send,
    pair_recv,
    w_send,
    w_recv,
    x_send,
    x_recv,
    y_send,
    y_recv,
    a_send,
    a_recv,
    s_send,
    s_recv,
    z_send,
    z_recv,
    g_send,
    g_recv,
    f_send,
    f_recv,
    r_send,
    r_recv,
    b_send,
    b_recv,
    h_send,
    h_recv,
):
    chunks = part.shape[0]
    groups = ny * nx * 2
    batch = deltas_ref.shape[0] // groups
    columns = w_ref.shape[0]
    me = lax.axis_index("emb")
    core = lax.rem(me, 2)
    at_x = lax.rem(me // 2, nx)
    at_y = me // (2 * nx)
    replica = lax.axis_index("dense")
    at_low = lax.rem(replica, 2)
    at_z = replica // 2

    def there(y, x, c):
        return {"emb": (lax.rem(y, ny) * nx + lax.rem(x, nx)) * 2 + c}

    sibling = there(at_y, at_x, 1 - core)
    x_next = there(at_y, at_x + 1, core)
    x_prev = there(at_y, at_x + nx - 1, core)
    y_next = there(at_y + 1, at_x, core)
    y_prev = there(at_y + ny - 1, at_x, core)
    y_far = there(at_y + 2, at_x, core)
    partner = {"dense": at_z * 2 + 1 - at_low}

    def away(k):
        return lax.rem(at_z + k, nz)

    def peer(k):
        return {"dense": away(k) * 2 + at_low}

    z_ends = (peer(1), peer(nz - 1))

    barrier = pltpu.get_barrier_semaphore()

    def greet(k, carry):
        pl.semaphore_signal(
            barrier, inc=1, device_id={"emb": lax.rem(me + k, groups)}, device_id_type=MESH
        )
        return carry

    def greet_z(k, carry):
        pl.semaphore_signal(barrier, inc=1, device_id=peer(k), device_id_type=MESH)
        return carry

    lax.fori_loop(1, groups, greet, 0)
    lax.fori_loop(1, nz, greet_z, 0)
    pl.semaphore_signal(barrier, inc=1, device_id=partner, device_id_type=MESH)

    spread[...] = deltas_ref[...].astype(F32).reshape(groups, batch, 128)
    for q in range(nx):
        for p in range(ny):
            block = (lax.rem(at_y + p, ny) * nx + lax.rem(at_x + q, nx)) * 2
            give[q * ny + p] = spread[block + 1 - core]
            left[pl.ds((q * ny + p) * batch, batch), :] = spread[block + core]
    w_give[...] = w_ref[...].astype(F32).reshape(w_give.shape)
    right[:, :, :128] = w_ref[...].reshape(chunks, CHUNK, 128)

    part_rows = tower.shape[2]
    spare = nz * 2 * part_rows - columns
    extra = jnp.where(
        lax.broadcasted_iota(jnp.int32, (spare, 128), 0) == 0,
        jnp.broadcast_to(bias_ref[...], (spare, 128)),
        0.0,
    )
    tower[...] = jnp.concatenate([wg_ref[...], extra], axis=0).reshape(tower.shape)

    pl.semaphore_wait(barrier, groups - 1 + nz)

    turns = nz // 2
    bit = part_rows // 2

    def ring_at(way, k):
        return away(k) if way == 0 else away(nz - k)

    def r_copy(s, h, way):
        return remote(
            tower.at[ring_at(way, turns - s), h],
            t_from.at[way, s, h],
            r_send.at[way, s, h],
            r_recv.at[way, s, h],
            z_ends[way],
        )

    def r_first(h, way):
        rows = pl.ds(way * bit, bit)
        return remote(
            tower.at[away(turns), h, rows],
            t_from.at[way, 0, h, rows],
            r_send.at[way, 0, h],
            r_recv.at[way, 0, h],
            z_ends[way],
        )

    def b_copy(h):
        return remote(tower.at[at_z, h], t_swap.at[h], b_send.at[h], b_recv.at[h], partner)

    def h_copy(s, h, way):
        place = t_final.at[ring_at(1 - way, s), h]
        return remote(place, place, h_send.at[way, s, h], h_recv.at[way, s, h], z_ends[way])

    def h_last(h, way):
        place = t_final.at[ring_at(1 - way, turns - 1), h, pl.ds(way * bit, bit)]
        return remote(
            place,
            place,
            h_send.at[way, turns - 1, h],
            h_recv.at[way, turns - 1, h],
            z_ends[way],
        )

    def advance(n, carry):
        h = lax.rem(n, 2)
        s = n // 2

        @pl.when(s == 0)
        def _():
            for way in range(2):
                r_first(h, way).start()

        @pl.when(s == 1)
        def _():
            for way in range(2):
                r_first(h, way).wait_recv()
                t = ring_at(way, turns - 1)
                rows = pl.ds(way * bit, bit)
                tower[t, h, rows] = tower[t, h, rows] + t_from[way, 0, h, rows]
                r_copy(1, h, way).start()

        @pl.when(jnp.logical_and(s >= 2, s < turns))
        def _():
            for way in range(2):
                r_copy(s - 1, h, way).wait_recv()
                t = ring_at(way, turns - s)
                tower[t, h] = tower[t, h] + t_from[way, s - 1, h]
                r_copy(s, h, way).start()

        @pl.when(s == turns)
        def _():
            r_copy(turns - 1, h, 0).wait_recv()
            r_copy(turns - 1, h, 1).wait_recv()
            tower[at_z, h] = (
                tower[at_z, h] + t_from[0, turns - 1, h] + t_from[1, turns - 1, h]
            )
            b_copy(h).start()

        @pl.when(s == turns + 1)
        def _():
            b_copy(h).wait_recv()
            t_final[at_z, h] = tower[at_z, h] + t_swap[h]
            for way in range(2):
                h_copy(0, h, way).start()

        @pl.when(jnp.logical_and(s >= turns + 2, s < 2 * turns))
        def _():
            for way in range(2):
                h_copy(s - turns - 2, h, way).wait_recv()
                h_copy(s - turns - 1, h, way).start()

        @pl.when(s == 2 * turns)
        def _():
            for way in range(2):
                h_copy(turns - 2, h, way).wait_recv()
                h_last(h, way).start()

        @pl.when(s == 2 * turns + 1)
        def _():
            for way in range(2):
                h_last(h, way).wait_recv()

        return carry

    advances = 2 * (2 * turns + 2)

    def pair_copy():
        return remote(give, take, pair_send, pair_recv, sibling)

    def w_copy(j):
        return remote(w_give.at[j], w_take.at[j], w_send.at[j], w_recv.at[j], sibling)

    half = 2 * batch

    def x_copy(j, kind):
        if kind == 0:
            src, dst, where = part.at[j, 2, pl.ds(0, half)], relay.at[j, 0], x_next
        elif kind == 1:
            src, dst, where = part.at[j, 2, pl.ds(half, half)], relay.at[j, 1], x_prev
        elif kind == 2:
            src, dst, where = part.at[j, 1], from_x.at[j, 0], x_next
        else:
            src, dst, where = part.at[j, 3], from_x.at[j, 1], x_prev
        return remote(src, dst, x_send.at[kind, j], x_recv.at[kind, j], where)

    def y_copy(j, kind):
        where = (y_next, y_far, y_prev)[kind]
        src = part.at[j, 0, pl.ds((kind + 1) * batch, batch)]
        return remote(src, from_y.at[j, kind], y_send.at[kind, j], y_recv.at[kind, j], where)

    pair_copy().start()

    def w_start(j, carry):
        w_copy(j).start()
        return carry

    lax.fori_loop(0, chunks, w_start, 0)
    lax.fori_loop(0, 2, advance, 0)
    pair_copy().wait_recv()
    left_own = left[...].astype(BF16)
    left_pair = take[...].reshape(left.shape).astype(BF16)
    lead_s2, lead_y, lead_end = 3, 6, 9
    slots = groups * CAP
    slabs = 8
    slab = local_rows // slabs

    def first_advance(i):
        return jnp.minimum(2 + (4 * i) // 3, advances)

    def step(i, carry):
        @pl.when(i < chunks)
        def _():
            w_copy(i).wait_recv()
            right[i, :, 128:] = w_take[i].astype(BF16)
            product = lax.dot_general(
                jnp.concatenate([left_own, left_pair], axis=1),
                right[i],
                (((1,), (1,)), ((), ())),
                preferred_element_type=F32,
            )
            part[i] = product.reshape(part.shape[1:])
            x_copy(i, 0).start()
            x_copy(i, 1).start()

        @pl.when(jnp.logical_and(i >= lead_s2, i < chunks + lead_s2))
        def _():
            j = i - lead_s2
            x_copy(j, 0).wait_recv()
            part[j, 1, pl.ds(0, half)] = part[j, 1, pl.ds(0, half)] + relay[j, 0]
            x_copy(j, 2).start()
            x_copy(j, 1).wait_recv()
            part[j, 3, pl.ds(half, half)] = part[j, 3, pl.ds(half, half)] + relay[j, 1]
            x_copy(j, 3).start()

        lax.fori_loop(first_advance(i), first_advance(i + 1), advance, 0)

        @pl.when(i == 4)
        def _():
            placing[...] = place_rows(mine_ref[...], groups, local_rows)

        @pl.when(i == 6)
        def _():
            wide = jnp.broadcast_to(landing_rows(ids_ref[...], me, local_rows), (slots, 128))
            target[...] = wide.T[0:8].astype(jnp.int32)

        @pl.when(jnp.logical_and(i >= 7, i < 7 + slabs))
        def _():
            first = (i - 7) * slab
            rows = lax.broadcasted_iota(jnp.int32, (slab, slots), 0) + first
            landing[i - 7] = (rows == target[0:1]).astype(F32).astype(BF16)

        @pl.when(jnp.logical_and(i >= lead_y, i < chunks + lead_y))
        def _():
            j = i - lead_y
            x_copy(j, 2).wait_recv()
            x_copy(j, 3).wait_recv()
            part[j, 0] = part[j, 0] + from_x[j, 0] + from_x[j, 1]
            for kind in (1, 0, 2):
                y_copy(j, kind).start()

        @pl.when(i >= lead_end)
        def _():
            j = i - lead_end
            for kind in range(3):
                y_copy(j, kind).wait_recv()
            total = part[j, 0, pl.ds(0, batch)] + from_y[j, 0] + from_y[j, 1] + from_y[j, 2]
            for n in range(CHUNK // 128):
                grads[j * (CHUNK // 128) + n] = total[:, n * 128 : (n + 1) * 128]

        return carry

    lax.fori_loop(0, chunks + lead_end, step, 0)

    wide = halves(grads[...].reshape(-1, 128))
    both = jnp.dot(placing[...], wide, preferred_element_type=F32)
    out_rows[...] = (both[:, :128] + both[:, 128:]).reshape(out_rows.shape)

    def a_copy(k):
        owner = lax.rem(me + k, groups)
        return remote(
            out_rows.at[owner], in_rows.at[me], a_send.at[k], a_recv.at[k], {"emb": owner}
        )

    def a_start(k, carry):
        a_copy(lax.rem(k + 14, groups - 1) + 1).start()
        return carry

    lax.fori_loop(1, groups, a_start, 0)
    in_rows[me] = out_rows[me]
    lax.fori_loop(first_advance(chunks + lead_end), advances, advance, 0)

    def a_wait(k, carry):
        a_copy(k).wait_recv()
        return carry

    lax.fori_loop(1, groups, a_wait, 0)

    wide = halves(in_rows[...].reshape(slots, 128))
    both = jnp.dot(
        landing[...].reshape(local_rows, slots), wide, preferred_element_type=F32
    )
    row_grad = both[:, :128] + both[:, 128:]
    shard = sums.shape[1]
    unused = 2 * nz * shard - local_rows
    if unused:
        row_grad = jnp.concatenate([row_grad, jnp.zeros((unused, 128), F32)], axis=0)
    sums[...] = row_grad.reshape(sums.shape)

    def s_copy(k):
        return remote(
            sums.at[away(k) * 2 + 1 - at_low], swap.at[k], s_send.at[k], s_recv.at[k], partner
        )

    def z_copy(k):
        return remote(mixed.at[k], from_z.at[k], z_send.at[k], z_recv.at[k], peer(k))

    def g_copy(k):
        place = final.at[replica]
        return remote(place, place, g_send.at[k], g_recv.at[k], peer(k))

    def f_copy(k):
        place = final.at[away(nz - k) * 2 + at_low]
        return remote(place, place, f_send.at[k], f_recv.at[k], partner)

    order = sorted(range(nz), key=lambda k: -min(k, nz - k))
    for k in order:
        s_copy(k).start()
    for k in order:
        s_copy(k).wait_recv()
        mixed[k] = sums[away(k) * 2 + at_low] + swap[k]
        if k:
            z_copy(k).start()
    tower_ref[...] = t_final[...].reshape(nz * 2 * part_rows, 128)[: columns + 8]
    total = mixed[0]
    for k in order[::-1]:
        if k:
            z_copy(k).wait_recv()
            total = total + from_z[k]
    final[replica] = total
    for k in order:
        if k:
            g_copy(k).start()
    f_copy(0).start()

    def drain(j, carry):
        w_copy(j).wait_send()
        for kind in range(4):
            x_copy(j, kind).wait_send()
        for kind in range(3):
            y_copy(j, kind).wait_send()
        return carry

    def a_drain(k, carry):
        a_copy(k).wait_send()
        return carry

    def t_drain(h, carry):
        for way in range(2):
            r_first(h, way).wait_send()
            h_last(h, way).wait_send()
            h_copy(0, h, way).wait_send()
        b_copy(h).wait_send()

        def inner(s, carry):
            for way in range(2):
                r_copy(s, h, way).wait_send()
            return carry

        def inner_h(s, carry):
            for way in range(2):
                h_copy(s, h, way).wait_send()
            return carry

        lax.fori_loop(1, turns, inner, 0)
        lax.fori_loop(1, turns - 1, inner_h, 0)
        return carry

    pair_copy().wait_send()
    lax.fori_loop(0, chunks, drain, 0)
    lax.fori_loop(1, groups, a_drain, 0)
    lax.fori_loop(0, 2, t_drain, 0)
    for k in order[::-1]:
        if k:
            g_copy(k).wait_recv()
            f_copy(k).start()
    for k in order[::-1]:
        f_copy(k).wait_recv()
    for k in order:
        s_copy(k).wait_send()
        f_copy(k).wait_send()
        if k:
            z_copy(k).wait_send()
            g_copy(k).wait_send()
    total_ref[...] = final[...]


def step(deltas, tower_w, block_ids, ids, tower_grad, bias, local_rows, dense, ny, nx):
    samples = deltas.shape[0]
    groups = ny * nx * 2
    nz = dense // 2
    batch = samples // groups
    columns = tower_w.shape[0]
    chunks = columns // CHUNK
    entries = block_ids.shape[1]
    slots = groups * CAP
    shard = -(-local_rows // (dense * 8)) * 8
    piece = -(-(columns + 8) // (nz * 32)) * 16
    turns = nz // 2
    vmem = pltpu.VMEM
    dma = pltpu.SemaphoreType.DMA
    total, tower = pl.pallas_call(
        functools.partial(step_kernel, ny, nx, nz, local_rows),
        out_shape=(
            jax.ShapeDtypeStruct((dense, shard, 128), F32),
            jax.ShapeDtypeStruct((columns + 8, 128), F32),
        ),
        in_specs=[pl.BlockSpec(memory_space=vmem)] * 6,
        out_specs=[pl.BlockSpec(memory_space=vmem)] * 2,
        scratch_shapes=[
            vmem((groups, batch, 128), F32),
            vmem((nx * ny, batch, 128), F32),
            vmem((nx * ny, batch, 128), F32),
            vmem((chunks, CHUNK, 128), F32),
            vmem((chunks, CHUNK, 128), F32),
            vmem((nx * ny * batch, 128), F32),
            vmem((chunks, CHUNK, 256), BF16),
            vmem((chunks, nx, ny * batch, CHUNK), F32),
            vmem((chunks, 2, 2 * batch, CHUNK), F32),
            vmem((chunks, 2, ny * batch, CHUNK), F32),
            vmem((chunks, 3, batch, CHUNK), F32),
            vmem((columns // 128, batch, 128), F32),
            vmem((slots, entries), BF16),
            vmem((groups, CAP, 128), F32),
            vmem((groups, CAP, 128), F32),
            vmem((8, slots), jnp.int32),
            vmem((8, local_rows // 8, slots), BF16),
            vmem((dense, shard, 128), F32),
            vmem((nz, shard, 128), F32),
            vmem((nz, shard, 128), F32),
            vmem((nz, shard, 128), F32),
            vmem((dense, shard, 128), F32),
            vmem((nz, 2, piece, 128), F32),
            vmem((2, turns, 2, piece, 128), F32),
            vmem((2, piece, 128), F32),
            vmem((nz, 2, piece, 128), F32),
            dma,
            dma,
            dma((chunks,)),
            dma((chunks,)),
            dma((4, chunks)),
            dma((4, chunks)),
            dma((3, chunks)),
            dma((3, chunks)),
            dma((groups,)),
            dma((groups,)),
        ]
        + [dma((nz,))] * 8
        + [
            dma((2, turns, 2)),
            dma((2, turns, 2)),
            dma((2,)),
            dma((2,)),
            dma((2, turns, 2)),
            dma((2, turns, 2)),
        ],
        compiler_params=pltpu.CompilerParams(
            collective_id=0, has_side_effects=True, vmem_limit_bytes=58 << 20
        ),
        cost_estimate=pl.CostEstimate(flops=1 << 30, bytes_accessed=8 << 20, transcendentals=0),
    )(deltas, tower_w, block_ids, ids, tower_grad, bias)
    return total.reshape(dense * shard, 128), tower


def shards(pooled, upstream, preact, tower_w, row_ids, table, accum):
    groups = lax.axis_size("emb")
    dense = lax.axis_size("dense")
    local_rows = table.shape[0]
    slope = silu_slope(preact.astype(F32))
    deltas = (upstream.astype(F32) * slope).astype(BF16)
    weight_grad = lax.dot_general(
        pooled, deltas, (((0,), (0,)), ((), ())), preferred_element_type=F32
    )
    bias = jnp.sum(deltas.astype(F32), axis=0)[None, :]
    ids = row_ids.reshape(groups, -1, row_ids.shape[1]).transpose(0, 2, 1).reshape(groups, -1)
    block_ids = lax.dynamic_slice_in_dim(ids, lax.axis_index("emb"), 1, 0)
    total, tower = step(
        deltas, tower_w, block_ids, ids, weight_grad, bias, local_rows, dense, 4, 4
    )
    columns = tower_w.shape[0]
    row_grad = total[:local_rows]
    new_accum = accum + jnp.mean(row_grad * row_grad, axis=1)
    new_table = table - learn_rate * row_grad / jnp.sqrt(new_accum)[:, None]
    return (tower[:columns], tower[columns], new_table, new_accum)


def solution(mesh):
    placed = (
        P("dense", None),
        P("dense", "emb"),
        P("dense", "emb"),
        P(None, "emb"),
        P("dense", None),
        P("emb", None),
        P("emb"),
    )
    return jax.shard_map(
        shards,
        mesh=mesh,
        in_specs=placed,
        out_specs=(P(None, "emb"), P("emb"), P("emb", None), P("emb")),
        check_vma=False,
    )
```

time: 258 us -> 172 us (0.67)
  the two profiles are of different devices: /device:TPU:14 before, /device:TPU:8 now
where the time goes in v2:
time: 172 us
  Pallas kernels  155 us (90%)
  local copies, waits for them, and re-layouts  6.47 us (4%)
  matrix products  5.72 us (3%)
  other arithmetic  3.98 us (2%)
    pallas_call x1, Pallas kernels, step(): pl.pallas_call(functools.partial(step_kernel, ny, nx, nz, local_rows), ou...  155 us
    dot_general x1, matrix products, shards(): lax.dot_general(pooled, deltas, (((0,), (0,)), ((), ())), preferred_eleme...  5.72 us

profile of v2, /device:TPU:8, one launch (start us, length us, event | category | flops | bytes accessed | tf_op | source)
XLA Modules:
  0.0 171.9 jit_solution(14780358945145115900)
XLA Ops:
  0.6 1.7 %convert_reduce_fusion = (f32[128]{0:T(128)}, bf16[768,128]{1,0:T(8,128)(2,1)S(1)}) fusion(bf16[768,128]{1,0:T(8,128)(2,1)} %param.9, bf16[768,128]{1,0:T(8,128)(2,1)} %param.8), kind=kLoop, calls=%fused_computation.12 | loop fusion | flops 1277824 | bytes 590336 | tf_op jit(solution)/shard_map/reduce_sum | solution.py:624
  2.4 0.0 copy-start.2
  2.4 1.2 reshape.18
  3.6 0.3 copy.13
  3.9 0.2 reshape.19.ids_ref
  4.1 0.0 copy-start.3
  4.1 0.6 constant_dynamic-slice_fusion.mine_ref
  4.7 5.7 %convolution_bitcast_fusion.wg_ref = f32[3328,128]{1,0:T(8,128)} fusion(bf16[768,128]{1,0:T(8,128)(2,1)S(1)} %get-tuple-element.11.deltas_ref, bf16[768,3328]{1,0:T(8,128)(2,1)} %param.7), kind=kOutput, calls=%fused_computation | convolution fusion | flops 654311424 | bytes 7012352 | tf_op jit(solution)/shard_map/dot_general | solution.py:621
  10.4 0.0 copy-done.2
  10.4 0.0 copy-done.3
  10.5 155.0 %shard_map.102 = (f32[24,88,128]{2,1,0:T(8,128)}, f32[3336,128]{1,0:T(8,128)}) custom-call(bf16[768,128]{1,0:T(8,128)(2,1)} %copy-done.2, bf16[3328,128]{1,0:T(8,128)(2,1)} %w_ref.1, s32[1,624]{1,0:T(1,128)} %constant_dynamic-slice_fusion.mine_ref, s32[32,624]{1,0:T(8,128)} %copy-done.3, f32[3328,128]{1,0:T(8,128)} %convolution_bitcast_fusion.wg_ref, ...), custom_call_target="tpu_custom_call" | custom-call | flops 1073741824 | bytes 8388608 | tf_op jit(solution)/shard_map/pallas_call | solution.py:552
  165.5 0.0 copy-start
  165.5 1.3 slice_bitcast_fusion
  166.7 0.0 copy-start.4
  166.7 0.0 copy-start.1
  166.7 2.8 %slice.9 = f32[3328,128]{1,0:T(8,128)} slice(f32[3336,128]{1,0:T(8,128)} %get-tuple-element.6), slice={[0:3328], [0:128]} | slice | bytes 3407872 | tf_op jit(solution)/shard_map/slice | solution.py:634
  169.6 0.0 copy-done
  169.6 0.3 multiply_reduce_fusion
  169.9 0.0 copy-done.4
  169.9 0.6 fusion.7
  170.5 0.0 copy-done.1
  170.5 1.3 divide_subtract_fusion
Async XLA Ops:
  2.4 8.1 %copy-start.2 = (bf16[768,128]{1,0:T(8,128)(2,1)}, bf16[768,128]{1,0:T(8,128)(2,1)S(1)}, u32[]{:S(2)}) copy-start(bf16[768,128]{1,0:T(8,128)(2,1)S(1)} %get-tuple-element.11.deltas_ref) | copy-start | bytes 589828
  4.1 6.3 %copy-start.3 = (s32[32,624]{1,0:T(8,128)}, s32[32,624]{1,0:T(8,128)S(1)}, u32[]{:S(2)}) copy-start(s32[32,624]{1,0:T(8,128)S(1)} %reshape.19.ids_ref) | copy-start | bytes 239620
  165.5 4.1 %copy-start = (f32[24,88,128]{2,1,0:T(8,128)S(1)}, f32[24,88,128]{2,1,0:T(8,128)}, u32[]{:S(2)}) copy-start(f32[24,88,128]{2,1,0:T(8,128)} %get-tuple-element.7) | copy-start | bytes 3244036
  166.7 3.2 %copy-start.4 = (f32[2048]{0:T(1024)S(1)}, f32[2048]{0:T(1024)}, u32[]{:S(2)}) copy-start(f32[2048]{0:T(1024)} %param.13) | copy-start | bytes 24580
  166.7 3.8 %copy-start.1 = (f32[2048,128]{1,0:T(8,128)S(1)}, f32[2048,128]{1,0:T(8,128)}, u32[]{:S(2)}) copy-start(f32[2048,128]{1,0:T(8,128)} %param.12) | copy-start | bytes 3145732

commit v3 on v2

--- a/solution.py
+++ b/solution.py
@@ -74,14 +74,15 @@
     nx,
     nz,
     local_rows,
-    deltas_ref,
+    pooled_ref,
+    upstream_ref,
+    preact_ref,
     w_ref,
     mine_ref,
     ids_ref,
-    wg_ref,
-    bias_ref,
     total_ref,
     tower_ref,
+    pooled,
     spread,
     give,
     take,
@@ -103,6 +104,7 @@
     swap,
     mixed,
     from_z,
+    merge,
     final,
     tower,
     t_from,
@@ -132,10 +134,16 @@
     b_recv,
     h_send,
     h_recv,
+    q_send,
+    q_recv,
+    e_send,
+    e_recv,
+    in_sem,
+    out_sem,
 ):
     chunks = part.shape[0]
     groups = ny * nx * 2
-    batch = deltas_ref.shape[0] // groups
+    batch = upstream_ref.shape[0] // groups
     columns = w_ref.shape[0]
     me = lax.axis_index("emb")
     core = lax.rem(me, 2)
@@ -164,6 +172,8 @@
 
     z_ends = (peer(1), peer(nz - 1))
 
+    load = pltpu.make_async_copy(pooled_ref, pooled, in_sem)
+    load.start()
     barrier = pltpu.get_barrier_semaphore()
 
     def greet(k, carry):
@@ -180,7 +190,9 @@
     lax.fori_loop(1, nz, greet_z, 0)
     pl.semaphore_signal(barrier, inc=1, device_id=partner, device_id_type=MESH)
 
-    spread[...] = deltas_ref[...].astype(F32).reshape(groups, batch, 128)
+    slope = silu_slope(preact_ref[...].astype(F32))
+    deltas = (upstream_ref[...].astype(F32) * slope).astype(BF16).astype(F32)
+    spread[...] = deltas.reshape(groups, batch, 128)
     for q in range(nx):
         for p in range(ny):
             block = (lax.rem(at_y + p, ny) * nx + lax.rem(at_x + q, nx)) * 2
@@ -189,26 +201,21 @@
     w_give[...] = w_ref[...].astype(F32).reshape(w_give.shape)
     right[:, :, :128] = w_ref[...].reshape(chunks, CHUNK, 128)
 
-    part_rows = tower.shape[2]
-    spare = nz * 2 * part_rows - columns
-    extra = jnp.where(
-        lax.broadcasted_iota(jnp.int32, (spare, 128), 0) == 0,
-        jnp.broadcast_to(bias_ref[...], (spare, 128)),
-        0.0,
-    )
-    tower[...] = jnp.concatenate([wg_ref[...], extra], axis=0).reshape(tower.shape)
-
     pl.semaphore_wait(barrier, groups - 1 + nz)
 
     turns = nz // 2
+    part_rows = t_swap.shape[1]
     bit = part_rows // 2
+
+    def stretch(t, h, first=0, size=part_rows):
+        return pl.ds(pl.multiple_of((t * 2 + h) * part_rows + first, 8), size)
 
     def ring_at(way, k):
         return away(k) if way == 0 else away(nz - k)
 
     def r_copy(s, h, way):
         return remote(
-            tower.at[ring_at(way, turns - s), h],
+            tower.at[stretch(ring_at(way, turns - s), h)],
             t_from.at[way, s, h],
             r_send.at[way, s, h],
             r_recv.at[way, s, h],
@@ -218,7 +225,7 @@
     def r_first(h, way):
         rows = pl.ds(way * bit, bit)
         return remote(
-            tower.at[away(turns), h, rows],
+            tower.at[stretch(away(turns), h, way * bit, bit)],
             t_from.at[way, 0, h, rows],
             r_send.at[way, 0, h],
             r_recv.at[way, 0, h],
@@ -226,14 +233,15 @@
         )
 
     def b_copy(h):
-        return remote(tower.at[at_z, h], t_swap.at[h], b_send.at[h], b_recv.at[h], partner)
+        place = tower.at[stretch(at_z, h)]
+        return remote(place, t_swap.at[h], b_send.at[h], b_recv.at[h], partner)
 
     def h_copy(s, h, way):
-        place = t_final.at[ring_at(1 - way, s), h]
+        place = t_final.at[stretch(ring_at(1 - way, s), h)]
         return remote(place, place, h_send.at[way, s, h], h_recv.at[way, s, h], z_ends[way])
 
     def h_last(h, way):
-        place = t_final.at[ring_at(1 - way, turns - 1), h, pl.ds(way * bit, bit)]
+        place = t_final.at[stretch(ring_at(1 - way, turns - 1), h, way * bit, bit)]
         return remote(
             place,
             place,
@@ -257,7 +265,8 @@
                 r_first(h, way).wait_recv()
                 t = ring_at(way, turns - 1)
                 rows = pl.ds(way * bit, bit)
-                tower[t, h, rows] = tower[t, h, rows] + t_from[way, 0, h, rows]
+                here = stretch(t, h, way * bit, bit)
+                tower[here, :] = tower[here, :] + t_from[way, 0, h, rows]
                 r_copy(1, h, way).start()
 
         @pl.when(jnp.logical_and(s >= 2, s < turns))
@@ -265,22 +274,23 @@
             for way in range(2):
                 r_copy(s - 1, h, way).wait_recv()
                 t = ring_at(way, turns - s)
-                tower[t, h] = tower[t, h] + t_from[way, s - 1, h]
+                tower[stretch(t, h), :] = tower[stretch(t, h), :] + t_from[way, s - 1, h]
                 r_copy(s, h, way).start()
 
         @pl.when(s == turns)
         def _():
             r_copy(turns - 1, h, 0).wait_recv()
             r_copy(turns - 1, h, 1).wait_recv()
-            tower[at_z, h] = (
-                tower[at_z, h] + t_from[0, turns - 1, h] + t_from[1, turns - 1, h]
+            here = stretch(at_z, h)
+            tower[here, :] = (
+                tower[here, :] + t_from[0, turns - 1, h] + t_from[1, turns - 1, h]
             )
             b_copy(h).start()
 
         @pl.when(s == turns + 1)
         def _():
             b_copy(h).wait_recv()
-            t_final[at_z, h] = tower[at_z, h] + t_swap[h]
+            t_final[stretch(at_z, h), :] = tower[stretch(at_z, h), :] + t_swap[h]
             for way in range(2):
                 h_copy(0, h, way).start()
 
@@ -336,32 +346,53 @@
         return carry
 
     lax.fori_loop(0, chunks, w_start, 0)
-    lax.fori_loop(0, 2, advance, 0)
     pair_copy().wait_recv()
     left_own = left[...].astype(BF16)
     left_pair = take[...].reshape(left.shape).astype(BF16)
-    lead_s2, lead_y, lead_end = 3, 6, 9
+    ahead = 4
+    lead_s2, lead_y, lead_end = ahead, ahead + 3, ahead + 6
     slots = groups * CAP
-    slabs = 8
-    slab = local_rows // slabs
+    shard = swap.shape[1]
 
     def first_advance(i):
-        return jnp.minimum(2 + (4 * i) // 3, advances)
+        return jnp.minimum(2 + (3 * (i - ahead)) // 2, advances)
+
+    def multiply(i, carry):
+        w_copy(i).wait_recv()
+        right[i, :, 128:] = w_take[i].astype(BF16)
+        product = lax.dot_general(
+            jnp.concatenate([left_own, left_pair], axis=1),
+            right[i],
+            (((1,), (1,)), ((), ())),
+            preferred_element_type=F32,
+        )
+        part[i] = product.reshape(part.shape[1:])
+        x_copy(i, 0).start()
+        x_copy(i, 1).start()
+        return carry
+
+    lax.fori_loop(0, ahead, multiply, 0)
+
+    spare = tower.shape[0] - columns
+    every = spread[...].reshape(groups * batch, 128)
+    tower[pl.ds(columns, spare), :] = jnp.where(
+        lax.broadcasted_iota(jnp.int32, (spare, 128), 0) == 0,
+        jnp.broadcast_to(jnp.sum(every, axis=0, keepdims=True), (spare, 128)),
+        0.0,
+    )
+    turned = every.T.astype(BF16)
+    load.wait()
+    for j in range(chunks):
+        flat = jnp.dot(
+            turned, pooled[:, j * CHUNK : (j + 1) * CHUNK], preferred_element_type=F32
+        )
+        tower[j * CHUNK : (j + 1) * CHUNK, :] = flat.T
+    lax.fori_loop(0, 2, advance, 0)
 
     def step(i, carry):
         @pl.when(i < chunks)
         def _():
-            w_copy(i).wait_recv()
-            right[i, :, 128:] = w_take[i].astype(BF16)
-            product = lax.dot_general(
-                jnp.concatenate([left_own, left_pair], axis=1),
-                right[i],
-                (((1,), (1,)), ((), ())),
-                preferred_element_type=F32,
-            )
-            part[i] = product.reshape(part.shape[1:])
-            x_copy(i, 0).start()
-            x_copy(i, 1).start()
+            multiply(i, 0)
 
         @pl.when(jnp.logical_and(i >= lead_s2, i < chunks + lead_s2))
         def _():
@@ -375,7 +406,7 @@
 
         lax.fori_loop(first_advance(i), first_advance(i + 1), advance, 0)
 
-        @pl.when(i == 4)
+        @pl.when(i == 5)
         def _():
             placing[...] = place_rows(mine_ref[...], groups, local_rows)
 
@@ -384,11 +415,15 @@
             wide = jnp.broadcast_to(landing_rows(ids_ref[...], me, local_rows), (slots, 128))
             target[...] = wide.T[0:8].astype(jnp.int32)
 
-        @pl.when(jnp.logical_and(i >= 7, i < 7 + slabs))
-        def _():
-            first = (i - 7) * slab
-            rows = lax.broadcasted_iota(jnp.int32, (slab, slots), 0) + first
-            landing[i - 7] = (rows == target[0:1]).astype(F32).astype(BF16)
+        @pl.when(jnp.logical_and(i >= 7, i < 7 + nz))
+        def _():
+            n = i - 7
+            k = turns + jnp.where(lax.rem(n, 2) == 0, (n + 1) // 2, -((n + 1) // 2))
+            rows = lax.broadcasted_iota(jnp.int32, (shard, slots), 0)
+            for low in range(2):
+                owned = 1 - at_low if low == 0 else at_low
+                hit = rows + (away(k) * 2 + owned) * shard == target[0:1]
+                landing[n, pl.ds(low * shard, shard), :] = hit.astype(F32).astype(BF16)
 
         @pl.when(jnp.logical_and(i >= lead_y, i < chunks + lead_y))
         def _():
@@ -410,7 +445,7 @@
 
         return carry
 
-    lax.fori_loop(0, chunks + lead_end, step, 0)
+    lax.fori_loop(ahead, chunks + lead_end, step, 0)
 
     wide = halves(grads[...].reshape(-1, 128))
     both = jnp.dot(placing[...], wide, preferred_element_type=F32)
@@ -436,20 +471,30 @@
 
     lax.fori_loop(1, groups, a_wait, 0)
 
+    tower_out = pltpu.make_async_copy(t_final, tower_ref, out_sem)
+    tower_out.start()
+
+    hop = turns // 2
+    reach = turns - hop
+    cut = shard // 16 * 8
+    order = sorted(range(nz), key=lambda k: (-min(k, nz - k), k))
+    near = order[2 * reach - 1 :]
     wide = halves(in_rows[...].reshape(slots, 128))
-    both = jnp.dot(
-        landing[...].reshape(local_rows, slots), wide, preferred_element_type=F32
-    )
-    row_grad = both[:, :128] + both[:, 128:]
-    shard = sums.shape[1]
-    unused = 2 * nz * shard - local_rows
-    if unused:
-        row_grad = jnp.concatenate([row_grad, jnp.zeros((unused, 128), F32)], axis=0)
-    sums[...] = row_grad.reshape(sums.shape)
-
-    def s_copy(k):
+
+    def s_copy(n, k):
         return remote(
-            sums.at[away(k) * 2 + 1 - at_low], swap.at[k], s_send.at[k], s_recv.at[k], partner
+            sums.at[n, pl.ds(0, shard)], swap.at[k], s_send.at[k], s_recv.at[k], partner
+        )
+
+    def q_copy(side, j):
+        k = hop + j if side == 0 else nz - hop - j
+        if j == reach:
+            rows = pl.ds(0, cut) if side == 0 else pl.ds(cut, shard - cut)
+            src, dst = mixed.at[k, rows], merge.at[side, j, rows]
+        else:
+            src, dst = mixed.at[k], merge.at[side, j]
+        return remote(
+            src, dst, q_send.at[side, j], q_recv.at[side, j], peer(j if side == 0 else nz - j)
         )
 
     def z_copy(k):
@@ -459,29 +504,71 @@
         place = final.at[replica]
         return remote(place, place, g_send.at[k], g_recv.at[k], peer(k))
 
+    def e_copy(side, j):
+        place = final.at[away(nz - hop if side == 0 else hop) * 2 + at_low]
+        if j == reach:
+            place = place.at[pl.ds(0, cut) if side == 0 else pl.ds(cut, shard - cut)]
+        return remote(
+            place, place, e_send.at[side, j], e_recv.at[side, j], peer(j if side == 0 else nz - j)
+        )
+
     def f_copy(k):
         place = final.at[away(nz - k) * 2 + at_low]
         return remote(place, place, f_send.at[k], f_recv.at[k], partner)
 
-    order = sorted(range(nz), key=lambda k: -min(k, nz - k))
-    for k in order:
-        s_copy(k).start()
-    for k in order:
-        s_copy(k).wait_recv()
-        mixed[k] = sums[away(k) * 2 + at_low] + swap[k]
-        if k:
+    parts = 3 if nz % 3 == 0 else 2
+    size = nz // parts
+    for n in range(parts):
+        both = jnp.dot(
+            landing[n * size : (n + 1) * size].reshape(size * 2 * shard, slots),
+            wide,
+            preferred_element_type=F32,
+        )
+        sums[n * size : (n + 1) * size] = (both[:, :128] + both[:, 128:]).reshape(
+            size, 2 * shard, 128
+        )
+        for m in range(n * size, (n + 1) * size):
+            s_copy(m, order[m]).start()
+
+    for n, k in enumerate(order):
+        s_copy(n, k).wait_recv()
+        mixed[k] = sums[n, pl.ds(shard, shard), :] + swap[k]
+        if k == turns:
+            q_copy(0, reach).start()
+            q_copy(1, reach).start()
+        elif hop < k < turns:
+            q_copy(0, k - hop).start()
+        elif turns < k < nz - hop:
+            q_copy(1, nz - hop - k).start()
+        elif k not in (0, hop, nz - hop):
             z_copy(k).start()
-    tower_ref[...] = t_final[...].reshape(nz * 2 * part_rows, 128)[: columns + 8]
+        if n == max(2 * reach, nz - 4):
+            for side in range(2):
+                mid = (hop, nz - hop)[side]
+                for j in range(reach, 0, -1):
+                    q_copy(side, j).wait_recv()
+                    if j == reach:
+                        rows = pl.ds(0, cut) if side == 0 else pl.ds(cut, shard - cut)
+                        mixed[mid, rows] = mixed[mid, rows] + merge[side, j, rows]
+                    else:
+                        mixed[mid] = mixed[mid] + merge[side, j]
+                z_copy(mid).start()
     total = mixed[0]
-    for k in order[::-1]:
+    for k in near[::-1]:
         if k:
             z_copy(k).wait_recv()
             total = total + from_z[k]
     final[replica] = total
-    for k in order:
+    for k in near:
         if k:
             g_copy(k).start()
     f_copy(0).start()
+    for side in range(2):
+        mid = (hop, nz - hop)[side]
+        g_copy(mid).wait_recv()
+        for j in range(reach, 0, -1):
+            e_copy(side, j).start()
+        f_copy(mid).start()
 
     def drain(j, carry):
         w_copy(j).wait_send()
@@ -520,23 +607,81 @@
     lax.fori_loop(0, chunks, drain, 0)
     lax.fori_loop(1, groups, a_drain, 0)
     lax.fori_loop(0, 2, t_drain, 0)
-    for k in order[::-1]:
-        if k:
+    for k in near[::-1]:
+        if k not in (0, hop, nz - hop):
             g_copy(k).wait_recv()
             f_copy(k).start()
+    for j in range(1, reach):
+        for side in range(2):
+            e_copy(side, j).wait_recv()
+            f_copy(hop + j if side == 0 else nz - hop - j).start()
+    e_copy(0, reach).wait_recv()
+    e_copy(1, reach).wait_recv()
+    f_copy(turns).start()
     for k in order[::-1]:
         f_copy(k).wait_recv()
-    for k in order:
-        s_copy(k).wait_send()
+    for n, k in enumerate(order):
+        s_copy(n, k).wait_send()
         f_copy(k).wait_send()
-        if k:
+        if k and k in near:
             z_copy(k).wait_send()
             g_copy(k).wait_send()
+    for side in range(2):
+        for j in range(1, reach + 1):
+            q_copy(side, j).wait_send()
+            e_copy(side, j).wait_send()
+    tower_out.wait()
     total_ref[...] = final[...]
 
 
-def step(deltas, tower_w, block_ids, ids, tower_grad, bias, local_rows, dense, ny, nx):
-    samples = deltas.shape[0]
+def finish_kernel(total_ref, tower_ref, table_ref, accum_ref, weight_ref, new_table_ref, new_accum_ref, sem):
+    out = pltpu.make_async_copy(tower_ref.at[pl.ds(0, weight_ref.shape[0])], weight_ref, sem)
+    out.start()
+    diagonal = lax.broadcasted_iota(jnp.int32, (128, 128), 0) == lax.broadcasted_iota(
+        jnp.int32, (128, 128), 1
+    )
+    ones = jnp.ones((128, 128), F32)
+    for n in range(accum_ref.shape[0]):
+        rows = pl.ds(n * 128, 128)
+        row_grad = total_ref[rows, :]
+        terms = row_grad * row_grad * (1.0 / 128.0) + jnp.where(
+            diagonal, jnp.broadcast_to(accum_ref[n : n + 1, :], (128, 128)), 0.0
+        )
+        grown = jnp.dot(terms, ones, precision=lax.Precision.HIGHEST, preferred_element_type=F32)
+        new_table_ref[rows, :] = table_ref[rows, :] - learn_rate * row_grad / jnp.sqrt(grown)
+        new_accum_ref[n : n + 1, :] = jnp.sum(
+            jnp.where(diagonal, grown, 0.0), axis=0, keepdims=True
+        )
+    out.wait()
+
+
+def finish(total, tower, table, accum, columns):
+    vmem = pltpu.VMEM
+    return pl.pallas_call(
+        finish_kernel,
+        out_shape=(
+            jax.ShapeDtypeStruct((columns, 128), F32),
+            jax.ShapeDtypeStruct(table.shape, F32),
+            jax.ShapeDtypeStruct(accum.shape, F32),
+        ),
+        in_specs=[
+            pl.BlockSpec(memory_space=vmem),
+            pl.BlockSpec(memory_space=pl.ANY),
+            pl.BlockSpec(memory_space=vmem),
+            pl.BlockSpec(memory_space=vmem),
+        ],
+        out_specs=[
+            pl.BlockSpec(memory_space=pl.ANY),
+            pl.BlockSpec(memory_space=vmem),
+            pl.BlockSpec(memory_space=vmem),
+        ],
+        scratch_shapes=[pltpu.SemaphoreType.DMA],
+        compiler_params=pltpu.CompilerParams(vmem_limit_bytes=32 << 20),
+    )(total, tower, table, accum)
+
+
+def step(pooled, upstream, preact, tower_w, block_ids, ids, local_rows, dense, ny, nx):
+    samples = upstream.shape[0]
     groups = ny * nx * 2
     nz = dense // 2
     batch = samples // groups
@@ -553,11 +698,12 @@
         functools.partial(step_kernel, ny, nx, nz, local_rows),
         out_shape=(
             jax.ShapeDtypeStruct((dense, shard, 128), F32),
-            jax.ShapeDtypeStruct((columns + 8, 128), F32),
+            jax.ShapeDtypeStruct((nz * 2 * piece, 128), F32),
         ),
-        in_specs=[pl.BlockSpec(memory_space=vmem)] * 6,
-        out_specs=[pl.BlockSpec(memory_space=vmem)] * 2,
+        in_specs=[pl.BlockSpec(memory_space=pl.ANY)] + [pl.BlockSpec(memory_space=vmem)] * 5,
+        out_specs=[pl.BlockSpec(memory_space=vmem), pl.BlockSpec(memory_space=pl.ANY)],
         scratch_shapes=[
+            vmem(pooled.shape, BF16),
             vmem((groups, batch, 128), F32),
             vmem((nx * ny, batch, 128), F32),
             vmem((nx * ny, batch, 128), F32),
@@ -574,16 +720,17 @@
             vmem((groups, CAP, 128), F32),
             vmem((groups, CAP, 128), F32),
             vmem((8, slots), jnp.int32),
-            vmem((8, local_rows // 8, slots), BF16),
-            vmem((dense, shard, 128), F32),
+            vmem((nz, 2 * shard, slots), BF16),
+            vmem((nz, 2 * shard, 128), F32),
             vmem((nz, shard, 128), F32),
             vmem((nz, shard, 128), F32),
             vmem((nz, shard, 128), F32),
+            vmem((2, turns - turns // 2 + 1, shard, 128), F32),
             vmem((dense, shard, 128), F32),
-            vmem((nz, 2, piece, 128), F32),
+            vmem((nz * 2 * piece, 128), F32),
             vmem((2, turns, 2, piece, 128), F32),
             vmem((2, piece, 128), F32),
-            vmem((nz, 2, piece, 128), F32),
+            vmem((nz * 2 * piece, 128), F32),
             dma,
             dma,
             dma((chunks,)),
@@ -603,12 +750,14 @@
             dma((2,)),
             dma((2, turns, 2)),
             dma((2, turns, 2)),
-        ],
+        ]
+        + [dma((2, turns - turns // 2 + 1))] * 4
+        + [dma, dma],
         compiler_params=pltpu.CompilerParams(
             collective_id=0, has_side_effects=True, vmem_limit_bytes=58 << 20
         ),
         cost_estimate=pl.CostEstimate(flops=1 << 30, bytes_accessed=8 << 20, transcendentals=0),
-    )(deltas, tower_w, block_ids, ids, tower_grad, bias)
+    )(pooled, upstream, preact, tower_w, block_ids, ids)
     return total.reshape(dense * shard, 128), tower
 
 
@@ -616,22 +765,16 @@
     groups = lax.axis_size("emb")
     dense = lax.axis_size("dense")
     local_rows = table.shape[0]
-    slope = silu_slope(preact.astype(F32))
-    deltas = (upstream.astype(F32) * slope).astype(BF16)
-    weight_grad = lax.dot_general(
-        pooled, deltas, (((0,), (0,)), ((), ())), preferred_element_type=F32
-    )
-    bias = jnp.sum(deltas.astype(F32), axis=0)[None, :]
     ids = row_ids.reshape(groups, -1, row_ids.shape[1]).transpose(0, 2, 1).reshape(groups, -1)
     block_ids = lax.dynamic_slice_in_dim(ids, lax.axis_index("emb"), 1, 0)
     total, tower = step(
-        deltas, tower_w, block_ids, ids, weight_grad, bias, local_rows, dense, 4, 4
+        pooled, upstream, preact, tower_w, block_ids, ids, local_rows, dense, 4, 4
     )
     columns = tower_w.shape[0]
-    row_grad = total[:local_rows]
-    new_accum = accum + jnp.mean(row_grad * row_grad, axis=1)
-    new_table = table - learn_rate * row_grad / jnp.sqrt(new_accum)[:, None]
-    return (tower[:columns], tower[columns], new_table, new_accum)
+    weight_grad, new_table, new_accum = finish(
+        total, tower, table, accum.reshape(-1, 128), columns
+    )
+    return (weight_grad, tower[columns], new_table, new_accum.reshape(-1))
 
 
 def solution(mesh):

time: 172 us -> 145 us (0.84)
  the two profiles are of different devices: /device:TPU:8 before, /device:TPU:14 now
where the time goes in v3:
time: 145 us
  Pallas kernels  138 us (95%)
  local copies, waits for them, and re-layouts  5.53 us (4%)
    pallas_call x1, Pallas kernels, step(): pl.pallas_call(functools.partial(step_kernel, ny, nx, nz, local_rows), ou...  136 us

profile of v3, /device:TPU:14, one launch (start us, length us, event | category | flops | bytes accessed | tf_op | source)
XLA Modules:
  0.0 144.7 jit_solution(12598039575668980639)
XLA Ops:
  0.6 1.2 reshape.23
  1.8 0.3 copy.12
  2.1 0.2 reshape.24.ids_ref
  2.3 0.0 copy-start.4
  2.3 0.6 constant_dynamic-slice_fusion.mine_ref
  2.9 0.0 copy-done.4
  3.0 0.0 copy-start.2
  3.0 0.0 copy-start.3
  3.0 136.3 %shard_map.102 = (f32[24,88,128]{2,1,0:T(8,128)}, f32[3456,128]{1,0:T(8,128)}) custom-call(bf16[768,3328]{1,0:T(8,128)(2,1)} %pooled_ref.1, bf16[768,128]{1,0:T(8,128)(2,1)} %upstream_ref.1, bf16[768,128]{1,0:T(8,128)(2,1)} %preact_ref.1, bf16[3328,128]{1,0:T(8,128)(2,1)} %w_ref.1, s32[1,624]{1,0:T(1,128)} %constant_dynamic-slice_fusion.mine_ref, ...), custom_call_target="tpu_custom_call" | custom-call | flops 1073741824 | bytes 8388608 | tf_op jit(solution)/shard_map/pallas_call | solution.py:697
  139.3 0.0 copy-done.2
  139.3 0.0 copy-done.3
  139.3 0.0 copy-start
  139.3 1.5 %copy-done = f32[3456,128]{1,0:T(8,128)S(1)} copy-done((f32[3456,128]{1,0:T(8,128)S(1)}, f32[3456,128]{1,0:T(8,128)}, u32[]{:S(2)}) %copy-start) | copy-done | bytes 1769496
  140.8 0.0 copy-start.1
  140.8 1.2 copy-done.1
  142.0 2.2 %shard_map.103 = (f32[3328,128]{1,0:T(8,128)}, f32[2048,128]{1,0:T(8,128)}, f32[16,128]{1,0:T(8,128)}) custom-call(f32[2112,128]{1,0:T(8,128)S(1)} %bitcast.8, f32[3456,128]{1,0:T(8,128)S(1)} %copy-done, f32[2048,128]{1,0:T(8,128)S(1)} %copy-done.2, f32[16,128]{1,0:T(8,128)S(1)} %bitcast.9), custom_call_target="tpu_custom_call" | custom-call | tf_op jit(solution)/shard_map/pallas_call | solution.py:660
  144.2 0.5 slice_bitcast_fusion
Async XLA Ops:
  2.3 0.6 copy-start.4
  3.0 136.3 %copy-start.2 = (f32[2048,128]{1,0:T(8,128)S(1)}, f32[2048,128]{1,0:T(8,128)}, u32[]{:S(2)}) copy-start(f32[2048,128]{1,0:T(8,128)} %table_ref.1) | copy-start | bytes 3145732
  3.0 136.3 %copy-start.3 = (f32[2048]{0:T(1024)S(1)}, f32[2048]{0:T(1024)}, u32[]{:S(2)}) copy-start(f32[2048]{0:T(1024)} %param.13) | copy-start | bytes 24580
  139.3 1.5 %copy-start = (f32[3456,128]{1,0:T(8,128)S(1)}, f32[3456,128]{1,0:T(8,128)}, u32[]{:S(2)}) copy-start(f32[3456,128]{1,0:T(8,128)} %get-tuple-element.10.tower_ref) | copy-start | bytes 5308420
  140.8 1.2 copy-start.1

commit v4 on v3

--- a/solution.py
+++ b/solution.py
@@ -78,7 +78,6 @@
     upstream_ref,
     preact_ref,
     w_ref,
-    mine_ref,
     ids_ref,
     total_ref,
     tower_ref,
@@ -89,6 +88,7 @@
     w_give,
     w_take,
     left,
+    lhs,
     right,
     part,
     relay,
@@ -157,11 +157,15 @@
         return {"emb": (lax.rem(y, ny) * nx + lax.rem(x, nx)) * 2 + c}
 
     sibling = there(at_y, at_x, 1 - core)
-    x_next = there(at_y, at_x + 1, core)
-    x_prev = there(at_y, at_x + nx - 1, core)
-    y_next = there(at_y + 1, at_x, core)
-    y_prev = there(at_y + ny - 1, at_x, core)
-    y_far = there(at_y + 2, at_x, core)
+
+    ahead = 4
+
+    def y_first(j):
+        return lax.rem(j, 2) * ((chunks + ahead - 1 - j) // chunks)
+
+    def along(turned, k):
+        return there(at_y + turned * k, at_x + (1 - turned) * k, core)
+
     partner = {"dense": at_z * 2 + 1 - at_low}
 
     def away(k):
@@ -325,17 +329,18 @@
 
     def x_copy(j, kind):
         if kind == 0:
-            src, dst, where = part.at[j, 2, pl.ds(0, half)], relay.at[j, 0], x_next
+            src, dst = part.at[j, 2, pl.ds(0, half)], relay.at[j, 0]
         elif kind == 1:
-            src, dst, where = part.at[j, 2, pl.ds(half, half)], relay.at[j, 1], x_prev
+            src, dst = part.at[j, 2, pl.ds(half, half)], relay.at[j, 1]
         elif kind == 2:
-            src, dst, where = part.at[j, 1], from_x.at[j, 0], x_next
+            src, dst = part.at[j, 1], from_x.at[j, 0]
         else:
-            src, dst, where = part.at[j, 3], from_x.at[j, 1], x_prev
+            src, dst = part.at[j, 3], from_x.at[j, 1]
+        where = along(y_first(j), 3 if kind % 2 else 1)
         return remote(src, dst, x_send.at[kind, j], x_recv.at[kind, j], where)
 
     def y_copy(j, kind):
-        where = (y_next, y_far, y_prev)[kind]
+        where = along(1 - y_first(j), kind + 1)
         src = part.at[j, 0, pl.ds((kind + 1) * batch, batch)]
         return remote(src, from_y.at[j, kind], y_send.at[kind, j], y_recv.at[kind, j], where)
 
@@ -347,9 +352,14 @@
 
     lax.fori_loop(0, chunks, w_start, 0)
     pair_copy().wait_recv()
-    left_own = left[...].astype(BF16)
-    left_pair = take[...].reshape(left.shape).astype(BF16)
-    ahead = 4
+    for n in range(2):
+        blocks = [q * ny + p for q in range(nx) for p in range(ny)]
+        if n:
+            blocks = [q * ny + p for p in range(ny) for q in range(nx)]
+        own = jnp.concatenate([left[k * batch : (k + 1) * batch] for k in blocks], axis=0)
+        pair = jnp.concatenate([take[k] for k in blocks], axis=0)
+        lhs[n, :, :128] = own.astype(BF16)
+        lhs[n, :, 128:] = pair.astype(BF16)
     lead_s2, lead_y, lead_end = ahead, ahead + 3, ahead + 6
     slots = groups * CAP
     shard = swap.shape[1]
@@ -361,7 +371,7 @@
         w_copy(i).wait_recv()
         right[i, :, 128:] = w_take[i].astype(BF16)
         product = lax.dot_general(
-            jnp.concatenate([left_own, left_pair], axis=1),
+            lhs[y_first(i)],
             right[i],
             (((1,), (1,)), ((), ())),
             preferred_element_type=F32,
@@ -408,7 +418,7 @@
 
         @pl.when(i == 5)
         def _():
-            placing[...] = place_rows(mine_ref[...], groups, local_rows)
+            placing[...] = place_rows(ids_ref[pl.ds(me, 1), :], groups, local_rows)
 
         @pl.when(i == 6)
         def _():
@@ -634,13 +644,38 @@
     total_ref[...] = final[...]
 
 
-def finish_kernel(total_ref, tower_ref, table_ref, accum_ref, weight_ref, new_table_ref, new_accum_ref, sem):
-    out = pltpu.make_async_copy(tower_ref.at[pl.ds(0, weight_ref.shape[0])], weight_ref, sem)
-    out.start()
+def finish_kernel(
+    total_hbm,
+    tower_hbm,
+    table_hbm,
+    accum_ref,
+    weight_ref,
+    new_table_ref,
+    new_accum_ref,
+    bias_ref,
+    total_ref,
+    table_ref,
+    tower_ref,
+    sems,
+):
+    columns = weight_ref.shape[0]
+    local_rows = table_ref.shape[0]
+    out = pltpu.make_async_copy(tower_ref.at[pl.ds(0, columns)], weight_ref, sems.at[0])
+    loads = [
+        pltpu.make_async_copy(tower_hbm.at[pl.ds(0, columns + 8)], tower_ref, sems.at[3]),
+        pltpu.make_async_copy(total_hbm.at[pl.ds(0, local_rows)], total_ref, sems.at[1]),
+        pltpu.make_async_copy(table_hbm, table_ref, sems.at[2]),
+    ]
+    for load in loads:
+        load.start()
     diagonal = lax.broadcasted_iota(jnp.int32, (128, 128), 0) == lax.broadcasted_iota(
         jnp.int32, (128, 128), 1
     )
     ones = jnp.ones((128, 128), F32)
+    for load in loads:
+        load.wait()
+    out.start()
+    bias_ref[...] = tower_ref[pl.ds(columns, 1), :]
     for n in range(accum_ref.shape[0]):
         rows = pl.ds(n * 128, 128)
         row_grad = total_ref[rows, :]
@@ -663,31 +698,28 @@
             jax.ShapeDtypeStruct((columns, 128), F32),
             jax.ShapeDtypeStruct(table.shape, F32),
             jax.ShapeDtypeStruct(accum.shape, F32),
+            jax.ShapeDtypeStruct((1, 128), F32),
         ),
-        in_specs=[
-            pl.BlockSpec(memory_space=vmem),
-            pl.BlockSpec(memory_space=pl.ANY),
-            pl.BlockSpec(memory_space=vmem),
-            pl.BlockSpec(memory_space=vmem),
+        in_specs=[pl.BlockSpec(memory_space=pl.ANY)] * 3 + [pl.BlockSpec(memory_space=vmem)],
+        out_specs=[pl.BlockSpec(memory_space=pl.ANY)] + [pl.BlockSpec(memory_space=vmem)] * 3,
+        scratch_shapes=[
+            vmem(table.shape, F32),
+            vmem(table.shape, F32),
+            vmem((columns + 8, 128), F32),
+            pltpu.SemaphoreType.DMA((4,)),
         ],
-        out_specs=[
-            pl.BlockSpec(memory_space=pl.ANY),
-            pl.BlockSpec(memory_space=vmem),
-            pl.BlockSpec(memory_space=vmem),
-        ],
-        scratch_shapes=[pltpu.SemaphoreType.DMA],
-        compiler_params=pltpu.CompilerParams(vmem_limit_bytes=32 << 20),
+        compiler_params=pltpu.CompilerParams(vmem_limit_bytes=58 << 20),
     )(total, tower, table, accum)
 
 
-def step(pooled, upstream, preact, tower_w, block_ids, ids, local_rows, dense, ny, nx):
+def step(pooled, upstream, preact, tower_w, ids, local_rows, dense, ny, nx):
     samples = upstream.shape[0]
     groups = ny * nx * 2
     nz = dense // 2
     batch = samples // groups
     columns = tower_w.shape[0]
     chunks = columns // CHUNK
-    entries = block_ids.shape[1]
+    entries = ids.shape[1]
     slots = groups * CAP
     shard = -(-local_rows // (dense * 8)) * 8
     piece = -(-(columns + 8) // (nz * 32)) * 16
@@ -700,7 +732,7 @@
             jax.ShapeDtypeStruct((dense, shard, 128), F32),
             jax.ShapeDtypeStruct((nz * 2 * piece, 128), F32),
         ),
-        in_specs=[pl.BlockSpec(memory_space=pl.ANY)] + [pl.BlockSpec(memory_space=vmem)] * 5,
+        in_specs=[pl.BlockSpec(memory_space=pl.ANY)] + [pl.BlockSpec(memory_space=vmem)] * 4,
         out_specs=[pl.BlockSpec(memory_space=vmem), pl.BlockSpec(memory_space=pl.ANY)],
         scratch_shapes=[
             vmem(pooled.shape, BF16),
@@ -710,6 +742,7 @@
             vmem((chunks, CHUNK, 128), F32),
             vmem((chunks, CHUNK, 128), F32),
             vmem((nx * ny * batch, 128), F32),
+            vmem((2, nx * ny * batch, 256), BF16),
             vmem((chunks, CHUNK, 256), BF16),
             vmem((chunks, nx, ny * batch, CHUNK), F32),
             vmem((chunks, 2, 2 * batch, CHUNK), F32),
@@ -757,7 +790,7 @@
             collective_id=0, has_side_effects=True, vmem_limit_bytes=58 << 20
         ),
         cost_estimate=pl.CostEstimate(flops=1 << 30, bytes_accessed=8 << 20, transcendentals=0),
-    )(pooled, upstream, preact, tower_w, block_ids, ids)
+    )(pooled, upstream, preact, tower_w, ids)
     return total.reshape(dense * shard, 128), tower
 
 
@@ -766,15 +799,14 @@
     dense = lax.axis_size("dense")
     local_rows = table.shape[0]
     ids = row_ids.reshape(groups, -1, row_ids.shape[1]).transpose(0, 2, 1).reshape(groups, -1)
-    block_ids = lax.dynamic_slice_in_dim(ids, lax.axis_index("emb"), 1, 0)
     total, tower = step(
-        pooled, upstream, preact, tower_w, block_ids, ids, local_rows, dense, 4, 4
+        pooled, upstream, preact, tower_w, ids, local_rows, dense, 4, 4
     )
     columns = tower_w.shape[0]
-    weight_grad, new_table, new_accum = finish(
+    weight_grad, new_table, new_accum, bias_grad = finish(
         total, tower, table, accum.reshape(-1, 128), columns
     )
-    return (weight_grad, tower[columns], new_table, new_accum.reshape(-1))
+    return (weight_grad, bias_grad.reshape(-1), new_table, new_accum.reshape(-1))
 
 
 def solution(mesh):

time: 145 us -> 144 us (level)
  the two profiles are of different devices: /device:TPU:14 before, /device:TPU:58 now
where the time goes in v4:
time: 144 us
  Pallas kernels  141 us (98%)
  local copies, waits for them, and re-layouts  2.31 us (2%)
    pallas_call x1, Pallas kernels, step(): pl.pallas_call(functools.partial(step_kernel, ny, nx, nz, local_rows), ou...  136 us
    pallas_call x1, Pallas kernels, finish(): pl.pallas_call(finish_kernel, out_shape=(jax.ShapeDtypeStruct((columns, 1...  4.95 us

profile of v4, /device:TPU:58, one launch (start us, length us, event | category | flops | bytes accessed | tf_op | source)
XLA Modules:
  0.0 143.9 jit_solution(11931404713258565119)
XLA Ops:
  0.6 1.2 reshape.26
  1.8 0.3 copy.12
  2.1 0.9 reshape.27.ids_ref
  3.0 136.0 %shard_map.102 = (f32[24,88,128]{2,1,0:T(8,128)}, f32[3456,128]{1,0:T(8,128)}) custom-call(bf16[768,3328]{1,0:T(8,128)(2,1)} %pooled_ref.1, bf16[768,128]{1,0:T(8,128)(2,1)} %upstream_ref.1, bf16[768,128]{1,0:T(8,128)(2,1)} %preact_ref.1, bf16[3328,128]{1,0:T(8,128)(2,1)} %w_ref.1, s32[32,624]{1,0:T(8,128)} %reshape.27.ids_ref), custom_call_target="tpu_custom_call" | custom-call | flops 1073741824 | bytes 8388608 | tf_op jit(solution)/shard_map/pallas_call | solution.py:729
  139.0 4.9 %shard_map.103 = (f32[3328,128]{1,0:T(8,128)}, f32[2048,128]{1,0:T(8,128)}, f32[16,128]{1,0:T(8,128)}, f32[1,128]{1,0:T(1,128)}) custom-call(f32[2112,128]{1,0:T(8,128)} %bitcast.8, f32[3456,128]{1,0:T(8,128)} %get-tuple-element.11.tower_hbm, f32[2048,128]{1,0:T(8,128)} %table_hbm.1, f32[16,128]{1,0:T(8,128)} %bitcast.9), custom_call_target="tpu_custom_call" | custom-call | tf_op jit(solution)/shard_map/pallas_call | solution.py:695

commit v5 on v4

--- a/solution.py
+++ b/solution.py
@@ -365,7 +365,7 @@
     shard = swap.shape[1]
 
     def first_advance(i):
-        return jnp.minimum(2 + (3 * (i - ahead)) // 2, advances)
+        return jnp.minimum(2 + (4 * (jnp.minimum(i, ahead + chunks) - ahead)) // 3, advances)
 
     def multiply(i, carry):
         w_copy(i).wait_recv()
@@ -647,34 +647,40 @@
 def finish_kernel(
     total_hbm,
     tower_hbm,
-    table_hbm,
+    table_ref,
     accum_ref,
     weight_ref,
     new_table_ref,
     new_accum_ref,
     bias_ref,
     total_ref,
-    table_ref,
     tower_ref,
     sems,
 ):
     columns = weight_ref.shape[0]
     local_rows = table_ref.shape[0]
-    out = pltpu.make_async_copy(tower_ref.at[pl.ds(0, columns)], weight_ref, sems.at[0])
-    loads = [
-        pltpu.make_async_copy(tower_hbm.at[pl.ds(0, columns + 8)], tower_ref, sems.at[3]),
-        pltpu.make_async_copy(total_hbm.at[pl.ds(0, local_rows)], total_ref, sems.at[1]),
-        pltpu.make_async_copy(table_hbm, table_ref, sems.at[2]),
-    ]
+    piece = columns // 4
+    half = local_rows // 2
+    loads, outs = [], []
+    for n in range(4):
+        rows = pl.ds(n * piece, piece + 8 if n == 3 else piece)
+        loads.append(pltpu.make_async_copy(tower_hbm.at[rows], tower_ref.at[rows], sems.at[n]))
+        rows = pl.ds(n * piece, piece)
+        outs.append(pltpu.make_async_copy(tower_ref.at[rows], weight_ref.at[rows], sems.at[4 + n]))
+    for n in range(2):
+        rows = pl.ds(n * half, half)
+        loads.append(pltpu.make_async_copy(total_hbm.at[rows], total_ref.at[rows], sems.at[8 + n]))
     for load in loads:
         load.start()
     diagonal = lax.broadcasted_iota(jnp.int32, (128, 128), 0) == lax.broadcasted_iota(
         jnp.int32, (128, 128), 1
     )
     ones = jnp.ones((128, 128), F32)
-    for load in loads:
+    for load, out in zip(loads, outs):
         load.wait()
-    out.start()
+        out.start()
+    for load in loads[4:]:
+        load.wait()
     bias_ref[...] = tower_ref[pl.ds(columns, 1), :]
     for n in range(accum_ref.shape[0]):
         rows = pl.ds(n * 128, 128)
@@ -687,7 +693,8 @@
         new_accum_ref[n : n + 1, :] = jnp.sum(
             jnp.where(diagonal, grown, 0.0), axis=0, keepdims=True
         )
-    out.wait()
+    for out in outs:
+        out.wait()
 
 
 def finish(total, tower, table, accum, columns):
@@ -700,13 +707,12 @@
             jax.ShapeDtypeStruct(accum.shape, F32),
             jax.ShapeDtypeStruct((1, 128), F32),
         ),
-        in_specs=[pl.BlockSpec(memory_space=pl.ANY)] * 3 + [pl.BlockSpec(memory_space=vmem)],
+        in_specs=[pl.BlockSpec(memory_space=pl.ANY)] * 2 + [pl.BlockSpec(memory_space=vmem)] * 2,
         out_specs=[pl.BlockSpec(memory_space=pl.ANY)] + [pl.BlockSpec(memory_space=vmem)] * 3,
         scratch_shapes=[
             vmem(table.shape, F32),
-            vmem(table.shape, F32),
             vmem((columns + 8, 128), F32),
-            pltpu.SemaphoreType.DMA((4,)),
+            pltpu.SemaphoreType.DMA((10,)),
         ],
         compiler_params=pltpu.CompilerParams(vmem_limit_bytes=58 << 20),
     )(total, tower, table, accum)

time: 144 us -> 138 us (0.958)
  the two profiles are of different devices: /device:TPU:58 before, /device:TPU:70 now
where the time goes in v5:
time: 138 us
  Pallas kernels  135 us (98%)
  local copies, waits for them, and re-layouts  2.31 us (2%)
    pallas_call x1, Pallas kernels, step(): pl.pallas_call(functools.partial(step_kernel, ny, nx, nz, local_rows), ou...  130 us
    pallas_call x1, Pallas kernels, finish(): pl.pallas_call(finish_kernel, out_shape=(jax.ShapeDtypeStruct((columns, 1...  5.19 us

profile of v5, /device:TPU:70, one launch (start us, length us, event | category | flops | bytes accessed | tf_op | source)
XLA Modules:
  0.0 137.8 jit_solution(16481656614498150279)
XLA Ops:
  0.6 1.2 reshape.26
  1.8 0.3 copy.12
  2.1 0.9 reshape.27.ids_ref
  3.0 129.6 %shard_map.102 = (f32[24,88,128]{2,1,0:T(8,128)}, f32[3456,128]{1,0:T(8,128)}) custom-call(bf16[768,3328]{1,0:T(8,128)(2,1)} %pooled_ref.1, bf16[768,128]{1,0:T(8,128)(2,1)} %upstream_ref.1, bf16[768,128]{1,0:T(8,128)(2,1)} %preact_ref.1, bf16[3328,128]{1,0:T(8,128)(2,1)} %w_ref.1, s32[32,624]{1,0:T(8,128)} %reshape.27.ids_ref), custom_call_target="tpu_custom_call" | custom-call | flops 1073741824 | bytes 8388608 | tf_op jit(solution)/shard_map/pallas_call | solution.py:735
  132.6 5.2 %shard_map.103 = (f32[3328,128]{1,0:T(8,128)}, f32[2048,128]{1,0:T(8,128)}, f32[16,128]{1,0:T(8,128)}, f32[1,128]{1,0:T(1,128)}) custom-call(f32[2112,128]{1,0:T(8,128)} %bitcast.8, f32[3456,128]{1,0:T(8,128)} %get-tuple-element.11.tower_hbm, f32[2048,128]{1,0:T(8,128)} %table_ref.1, f32[16,128]{1,0:T(8,128)} %bitcast.9), custom_call_target="tpu_custom_call" | custom-call | tf_op jit(solution)/shard_map/pallas_call | solution.py:702

commit v6 on v5

--- a/solution.py
+++ b/solution.py
@@ -650,51 +650,58 @@
     table_ref,
     accum_ref,
     weight_ref,
-    new_table_ref,
+    new_table_hbm,
     new_accum_ref,
     bias_ref,
     total_ref,
+    fresh,
     tower_ref,
     sems,
 ):
     columns = weight_ref.shape[0]
     local_rows = table_ref.shape[0]
     piece = columns // 4
-    half = local_rows // 2
-    loads, outs = [], []
+    size = local_rows // 4
+    towers, totals, weights, tables = [], [], [], []
     for n in range(4):
+        rows = pl.ds(n * size, size)
+        totals.append(pltpu.make_async_copy(total_hbm.at[rows], total_ref.at[rows], sems.at[n]))
+        tables.append(pltpu.make_async_copy(fresh.at[rows], new_table_hbm.at[rows], sems.at[4 + n]))
         rows = pl.ds(n * piece, piece + 8 if n == 3 else piece)
-        loads.append(pltpu.make_async_copy(tower_hbm.at[rows], tower_ref.at[rows], sems.at[n]))
+        towers.append(pltpu.make_async_copy(tower_hbm.at[rows], tower_ref.at[rows], sems.at[8 + n]))
         rows = pl.ds(n * piece, piece)
-        outs.append(pltpu.make_async_copy(tower_ref.at[rows], weight_ref.at[rows], sems.at[4 + n]))
-    for n in range(2):
-        rows = pl.ds(n * half, half)
-        loads.append(pltpu.make_async_copy(total_hbm.at[rows], total_ref.at[rows], sems.at[8 + n]))
-    for load in loads:
-        load.start()
+        weights.append(
+            pltpu.make_async_copy(tower_ref.at[rows], weight_ref.at[rows], sems.at[12 + n])
+        )
+    for n in range(4):
+        totals[n].start()
+        towers[n].start()
     diagonal = lax.broadcasted_iota(jnp.int32, (128, 128), 0) == lax.broadcasted_iota(
         jnp.int32, (128, 128), 1
     )
     ones = jnp.ones((128, 128), F32)
-    for load, out in zip(loads, outs):
-        load.wait()
-        out.start()
-    for load in loads[4:]:
-        load.wait()
+    for n in range(4):
+        totals[n].wait()
+        for m in range(n * size // 128, (n + 1) * size // 128):
+            rows = pl.ds(m * 128, 128)
+            row_grad = total_ref[rows, :]
+            terms = row_grad * row_grad * (1.0 / 128.0) + jnp.where(
+                diagonal, jnp.broadcast_to(accum_ref[m : m + 1, :], (128, 128)), 0.0
+            )
+            grown = jnp.dot(
+                terms, ones, precision=lax.Precision.HIGHEST, preferred_element_type=F32
+            )
+            fresh[rows, :] = table_ref[rows, :] - learn_rate * row_grad / jnp.sqrt(grown)
+            new_accum_ref[m : m + 1, :] = jnp.sum(
+                jnp.where(diagonal, grown, 0.0), axis=0, keepdims=True
+            )
+        tables[n].start()
+        towers[n].wait()
+        weights[n].start()
     bias_ref[...] = tower_ref[pl.ds(columns, 1), :]
-    for n in range(accum_ref.shape[0]):
-        rows = pl.ds(n * 128, 128)
-        row_grad = total_ref[rows, :]
-        terms = row_grad * row_grad * (1.0 / 128.0) + jnp.where(
-            diagonal, jnp.broadcast_to(accum_ref[n : n + 1, :], (128, 128)), 0.0
-        )
-        grown = jnp.dot(terms, ones, precision=lax.Precision.HIGHEST, preferred_element_type=F32)
-        new_table_ref[rows, :] = table_ref[rows, :] - learn_rate * row_grad / jnp.sqrt(grown)
-        new_accum_ref[n : n + 1, :] = jnp.sum(
-            jnp.where(diagonal, grown, 0.0), axis=0, keepdims=True
-        )
-    for out in outs:
-        out.wait()
+    for n in range(4):
+        tables[n].wait()
+        weights[n].wait()
 
 
 def finish(total, tower, table, accum, columns):
@@ -708,11 +715,12 @@
             jax.ShapeDtypeStruct((1, 128), F32),
         ),
         in_specs=[pl.BlockSpec(memory_space=pl.ANY)] * 2 + [pl.BlockSpec(memory_space=vmem)] * 2,
-        out_specs=[pl.BlockSpec(memory_space=pl.ANY)] + [pl.BlockSpec(memory_space=vmem)] * 3,
+        out_specs=[pl.BlockSpec(memory_space=pl.ANY)] * 2 + [pl.BlockSpec(memory_space=vmem)] * 2,
         scratch_shapes=[
             vmem(table.shape, F32),
+            vmem(table.shape, F32),
             vmem((columns + 8, 128), F32),
-            pltpu.SemaphoreType.DMA((10,)),
+            pltpu.SemaphoreType.DMA((16,)),
         ],
         compiler_params=pltpu.CompilerParams(vmem_limit_bytes=58 << 20),
     )(total, tower, table, accum)

time: 138 us -> 138 us (level)
  no operation moved by 1% of the time
where the time goes in v6:
time: 138 us
  Pallas kernels  135 us (98%)
  local copies, waits for them, and re-layouts  2.31 us (2%)
    pallas_call x1, Pallas kernels, step(): pl.pallas_call(functools.partial(step_kernel, ny, nx, nz, local_rows), ou...  130 us
    pallas_call x1, Pallas kernels, finish(): pl.pallas_call(finish_kernel, out_shape=(jax.ShapeDtypeStruct((columns, 1...  5.41 us

profile of v6, /device:TPU:70, one launch (start us, length us, event | category | flops | bytes accessed | tf_op | source)
XLA Modules:
  0.0 138.0 jit_solution(17364843862393868218)
XLA Ops:
  0.6 1.2 reshape.26
  1.8 0.3 copy.12
  2.1 0.9 reshape.27.ids_ref
  3.0 129.6 %shard_map.102 = (f32[24,88,128]{2,1,0:T(8,128)}, f32[3456,128]{1,0:T(8,128)}) custom-call(bf16[768,3328]{1,0:T(8,128)(2,1)} %pooled_ref.1, bf16[768,128]{1,0:T(8,128)(2,1)} %upstream_ref.1, bf16[768,128]{1,0:T(8,128)(2,1)} %preact_ref.1, bf16[3328,128]{1,0:T(8,128)(2,1)} %w_ref.1, s32[32,624]{1,0:T(8,128)} %reshape.27.ids_ref), custom_call_target="tpu_custom_call" | custom-call | flops 1073741824 | bytes 8388608 | tf_op jit(solution)/shard_map/pallas_call | solution.py:743
  132.6 5.4 %shard_map.103 = (f32[3328,128]{1,0:T(8,128)}, f32[2048,128]{1,0:T(8,128)}, f32[16,128]{1,0:T(8,128)}, f32[1,128]{1,0:T(1,128)}) custom-call(f32[2112,128]{1,0:T(8,128)} %bitcast.8, f32[3456,128]{1,0:T(8,128)} %get-tuple-element.11.tower_hbm, f32[2048,128]{1,0:T(8,128)} %table_ref.1, f32[16,128]{1,0:T(8,128)} %bitcast.9), custom_call_target="tpu_custom_call" | custom-call | tf_op jit(solution)/shard_map/pallas_call | solution.py:709
